TPU v7x, 32 devices: a whole 2x2x4 slice. The times are simulated.
32 devices in a mesh: dp: 4 (over z), blk: 8 (over y, x, core).
Axes of the slice: x: 2, y: 2, z: 4, core: 2. Of those that a mesh axis runs over, the one named last changes fastest.
Arguments:
- tokens: bfloat16 [8192, 1152], P(('dp', 'blk')), may hold values from -6 to 6
- cond: bfloat16 [20, 1152], replicated, may hold values from -6 to 6
- segments: int32 [8192], P(('dp', 'blk')), may hold values from 0 to 19, as said below
- kept: int32 [4096], P(('dp', 'blk')), may hold values from 0 to 255, as said below
- cotangent: bfloat16 [8192, 1152], P(('dp', 'blk')), may hold values from -6 to 6
- ada_weight: bfloat16 [2, 1152, 6912], P(None, 'dp'), may hold values from -0.1875 to 0.1875
- ada_bias: bfloat16 [2, 6912], P(None, 'dp'), may hold values from -3 to 3
- qkv_weight: bfloat16 [2, 1152, 3456], P(None, 'dp'), may hold values from -0.1875 to 0.1875
- qv_bias: bfloat16 [2, 2304], P(None, 'dp'), may hold values from -3 to 3
- out_weight: bfloat16 [2, 1152, 1152], P(None, 'dp'), may hold values from -2 to 2
- out_bias: bfloat16 [2, 1152], P(None, 'dp'), may hold values from -3 to 3
- up_weight: bfloat16 [2, 1152, 4608], P(None, 'dp'), may hold values from -0.1875 to 0.1875
- up_bias: bfloat16 [2, 4608], P(None, 'dp'), may hold values from -3 to 3
- down_weight: bfloat16 [2, 4608, 1152], P(None, 'dp'), may hold values from -0.09375 to 0.09375
- down_bias: bfloat16 [2, 1152], P(None, 'dp'), may hold values from -3 to 3
Outputs:
- mid: float32 [8192, 1152], P(('dp', 'blk'))
- final: float32 [8192, 1152], P(('dp', 'blk'))
- grad_tokens: float32 [8192, 1152], P(('dp', 'blk'))
- grad_ada_weight: float32 [2, 1152, 6912], P(None, 'dp')
- grad_ada_bias: float32 [2, 6912], P(None, 'dp')
- grad_qkv_weight: float32 [2, 1152, 3456], P(None, 'dp')
- grad_qv_bias: float32 [2, 2304], P(None, 'dp')
- grad_out_weight: float32 [2, 1152, 1152], P(None, 'dp')
- grad_out_bias: float32 [2, 1152], P(None, 'dp')
- grad_up_weight: float32 [2, 1152, 4608], P(None, 'dp')
- grad_up_bias: float32 [2, 4608], P(None, 'dp')
- grad_down_weight: float32 [2, 4608, 1152], P(None, 'dp')
- grad_down_bias: float32 [2, 1152], P(None, 'dp')
Inputs may be any that keep to these rules, and one draw needn't show every extreme that they name: `segments`: each block of 2048 consecutive tokens (one index of dp, number g) holds images g * 5 to g * 5 + 4: first 1 images of 1024 tokens, then 4 of 256. Every device's 256 rows hold the same number of tokens of each image of its block, in a random order. `kept`: for each device in turn, 128 distinct numbers of its own rows, increasing: the tokens that pass through the second block.
All inputs are finite; a program needn't handle non-finite values.
Results may differ from a plain program's by a relative error of at most 0.025.
Values may be sent and summed in bfloat16 or wider, within the bound.
No kernel may reach another device: no remote copies, remote signals or barrier semaphores. Data moves between devices by JAX's collectives and lax.ppermute only.
A program may use at most 448 MiB of HBM per device.

v0:
```python
import jax
import jax.numpy as jnp
from jax import lax
from jax.sharding import PartitionSpec as P

HEADS = 16


epsilon = 1e-06
highest = lax.Precision.HIGHEST


def as_sent(shard):
    return jax.tree.map(lambda a: a.astype(jnp.bfloat16) if a.dtype == jnp.float32 else a, shard)


def norm_rows(values):
    centered = values - jnp.mean(values, axis=-1, keepdims=True)
    return centered * lax.rsqrt(jnp.mean(centered * centered, axis=-1, keepdims=True) + epsilon)


def modulate(residual, shift, scale):
    return norm_rows(residual) * (1.0 + scale) + shift


def to_heads(rows):
    return jnp.transpose(rows.reshape(rows.shape[0], HEADS, -1), (1, 2, 0))


def from_heads(heads):
    return jnp.transpose(heads, (2, 0, 1)).reshape(heads.shape[2], -1)


def shard_blocks(array, row_count):
    return jnp.moveaxis(
        array.reshape(array.shape[:-1] + (array.shape[-1] // row_count, row_count)), -2, 0
    )


def exp_scores(query_heads, key_heads, query_seg, key_seg):
    raw_scores = jnp.einsum(
        "hdq,hdk->hqk", query_heads, key_heads, preferred_element_type=jnp.float32
    )
    scores = raw_scores * key_heads.shape[1] ** (-0.5)
    same_image = query_seg[None, :, None] == key_seg[None, None, :]
    return jnp.where(same_image, jnp.exp(jnp.where(same_image, scores, 0.0)), 0.0)


def attend(query_heads, key_heads, value_heads, query_seg, seg_all):
    row_count = query_heads.shape[2]
    start_sums = (
        jnp.zeros((HEADS, row_count), jnp.float32),
        jnp.zeros(query_heads.shape, jnp.float32),
    )
    key_part = lax.all_gather(key_heads, "blk", axis=2, tiled=True)
    value_part = lax.all_gather(value_heads, "blk", axis=2, tiled=True)

    def attend_one_shard(inside, shard_items):
        key_block, value_block, seg_block = shard_items
        weights = exp_scores(query_heads, key_block, query_seg, seg_block)
        partial_sum = jnp.einsum(
            "hqk,hdk->hdq",
            weights.astype(jnp.bfloat16),
            value_block,
            preferred_element_type=jnp.float32,
        )
        return ((inside[0] + jnp.sum(weights, axis=-1), inside[1] + partial_sum), None)

    folded, unused = lax.scan(
        attend_one_shard,
        start_sums,
        (
            shard_blocks(key_part, row_count),
            shard_blocks(value_part, row_count),
            shard_blocks(seg_all, row_count),
        ),
    )
    totals, summed = folded
    return (summed / totals[:, None, :], totals)


def query_grads(query_heads, carried, row_delta, query_seg, key_heads, value_heads, seg_all):
    row_count = query_heads.shape[2]
    score_scale = query_heads.shape[1] ** (-0.5)
    start_sum = jnp.zeros(query_heads.shape, jnp.float32)
    key_part = lax.all_gather(key_heads, "blk", axis=2, tiled=True)
    value_part = lax.all_gather(value_heads, "blk", axis=2, tiled=True)

    def query_one_shard(inside, shard_items):
        key_block, value_block, seg_block = shard_items
        weights = exp_scores(query_heads, key_block, query_seg, seg_block)
        products = jnp.einsum(
            "hdq,hdk->hqk", carried, value_block, preferred_element_type=jnp.float32
        )
        raw_grad = (weights * (products - row_delta[:, :, None]) * score_scale).astype(jnp.bfloat16)
        added = jnp.einsum("hqk,hdk->hdq", raw_grad, key_block, preferred_element_type=jnp.float32)
        return (inside + added, None)

    folded, unused = lax.scan(
        query_one_shard,
        start_sum,
        (
            shard_blocks(key_part, row_count),
            shard_blocks(value_part, row_count),
            shard_blocks(seg_all, row_count),
        ),
    )
    return folded


def key_grads(key_heads, value_heads, key_seg, query_heads, carried, seg_all, delta_all):
    row_count = key_heads.shape[2]
    score_scale = key_heads.shape[1] ** (-0.5)
    start_sums = (jnp.zeros(key_heads.shape, jnp.float32), jnp.zeros(key_heads.shape, jnp.float32))
    query_part = lax.all_gather(query_heads, "blk", axis=2, tiled=True)
    carried_part = lax.all_gather(carried, "blk", axis=2, tiled=True)

    def key_one_shard(inside, shard_items):
        query_block, carried_block, seg_block, delta_block = shard_items
        weights = exp_scores(query_block, key_heads, seg_block, key_seg)
        products = jnp.einsum(
            "hdq,hdk->hqk", carried_block, value_heads, preferred_element_type=jnp.float32
        )
        raw_grad = (weights * (products - delta_block[:, :, None]) * score_scale).astype(
            jnp.bfloat16
        )
        key_sum = jnp.einsum(
            "hqk,hdq->hdk", raw_grad, query_block, preferred_element_type=jnp.float32
        )
        value_sum = jnp.einsum(
            "hqk,hdq->hdk",
            weights.astype(jnp.bfloat16),
            carried_block,
            preferred_element_type=jnp.float32,
        )
        return ((inside[0] + key_sum, inside[1] + value_sum), None)

    folded, unused = lax.scan(
        key_one_shard,
        start_sums,
        (
            shard_blocks(query_part, row_count),
            shard_blocks(carried_part, row_count),
            shard_blocks(seg_all, row_count),
            shard_blocks(delta_all, row_count),
        ),
    )
    return folded


def fetch_block(layer_index, params):
    (
        ada_weight,
        ada_bias,
        qkv_weight,
        qv_bias,
        out_weight,
        out_bias,
        up_weight,
        up_bias,
        down_weight,
        down_bias,
    ) = params
    return tuple(
        (
            lax.all_gather(ada_weight[layer_index], "dp", axis=0, tiled=True),
            lax.all_gather(ada_bias[layer_index], "dp", axis=0, tiled=True),
            lax.all_gather(qkv_weight[layer_index], "dp", axis=0, tiled=True),
            lax.all_gather(qv_bias[layer_index], "dp", axis=0, tiled=True),
            lax.all_gather(out_weight[layer_index], "dp", axis=0, tiled=True),
            lax.all_gather(out_bias[layer_index], "dp", axis=0, tiled=True),
            lax.all_gather(up_weight[layer_index], "dp", axis=0, tiled=True),
            lax.all_gather(up_bias[layer_index], "dp", axis=0, tiled=True),
            lax.all_gather(down_weight[layer_index], "dp", axis=0, tiled=True),
            lax.all_gather(down_bias[layer_index], "dp", axis=0, tiled=True),
        )
    )


def modulation(weights, placing):
    silu_cond, image_start, image_count, shard_start = placing
    ada_weight, ada_bias = (weights[0], weights[1])
    local_cond = lax.dynamic_slice_in_dim(silu_cond, image_start, image_count, 0)
    return jnp.dot(local_cond, ada_weight, preferred_element_type=jnp.float32) + ada_bias


def forward_block(weights, residual, local_images, placing, query_seg, seg_all):
    (
        ada_weight,
        ada_bias,
        qkv_weight,
        qv_bias,
        out_weight,
        out_bias,
        up_weight,
        up_bias,
        down_weight,
        down_bias,
    ) = weights
    features = residual.shape[1]
    mod_group = modulation(weights, placing)
    onehot = (
        local_images[:, None] == jnp.arange(mod_group.shape[0], dtype=jnp.int32)[None, :]
    ).astype(jnp.float32)
    per_token = jnp.dot(onehot, mod_group, precision=highest)
    shift_one, scale_one, gate_one, shift_two, scale_two, gate_two = jnp.split(per_token, 6, axis=1)
    first_in = modulate(residual, shift_one, scale_one).astype(jnp.bfloat16)
    joined = jnp.dot(first_in, qkv_weight, preferred_element_type=jnp.float32)
    query_heads = to_heads((joined[:, :features] + qv_bias[:features]).astype(jnp.bfloat16))
    key_heads = to_heads(joined[:, features : 2 * features].astype(jnp.bfloat16))
    value_heads = to_heads((joined[:, 2 * features :] + qv_bias[features:]).astype(jnp.bfloat16))
    attended_heads, totals = attend(query_heads, key_heads, value_heads, query_seg, seg_all)
    mixed_rows = from_heads(attended_heads).astype(jnp.bfloat16)
    branch = jnp.dot(mixed_rows, out_weight, preferred_element_type=jnp.float32) + out_bias
    middle = residual + gate_one * branch
    second = modulate(middle, shift_two, scale_two).astype(jnp.bfloat16)
    hidden = jnp.dot(second, up_weight, preferred_element_type=jnp.float32) + up_bias
    active = jax.nn.gelu(hidden, approximate=True).astype(jnp.bfloat16)
    output = jnp.dot(active, down_weight, preferred_element_type=jnp.float32) + down_bias
    stored = (
        residual,
        onehot,
        per_token,
        first_in,
        query_heads,
        key_heads,
        value_heads,
        attended_heads,
        totals,
        mixed_rows,
        branch,
        middle,
        second,
        hidden,
        active,
        output,
    )
    return (middle + gate_two * output, stored)


def backward_block(weights, stored, grad_out, placing, query_seg, seg_all):
    (
        ada_weight,
        ada_bias,
        qkv_weight,
        qv_bias,
        out_weight,
        out_bias,
        up_weight,
        up_bias,
        down_weight,
        down_bias,
    ) = weights
    silu_cond, image_start, image_count, shard_start = placing
    (
        residual,
        onehot,
        per_token,
        first_in,
        query_heads,
        key_heads,
        value_heads,
        attended_heads,
        totals,
        mixed_rows,
        branch,
        middle,
        second,
        hidden,
        active,
        output,
    ) = stored
    shift_one, scale_one, gate_one, shift_two, scale_two, gate_two = jnp.split(per_token, 6, axis=1)
    row_count, features = residual.shape
    grad_gate_two = grad_out * output
    grad_output = (gate_two * grad_out).astype(jnp.bfloat16)
    grad_down = jnp.einsum("rk,rd->kd", active, grad_output, preferred_element_type=jnp.float32)
    grad_down_bias = jnp.sum(grad_output.astype(jnp.float32), axis=0)
    grad_active = jnp.einsum(
        "rd,kd->rk", grad_output, down_weight, preferred_element_type=jnp.float32
    )
    unused, gelu_pull = jax.vjp(lambda inner: jax.nn.gelu(inner, approximate=True), hidden)
    grad_hidden = gelu_pull(grad_active)[0].astype(jnp.bfloat16)
    grad_up = jnp.einsum("rk,rh->kh", second, grad_hidden, preferred_element_type=jnp.float32)
    grad_up_bias = jnp.sum(grad_hidden.astype(jnp.float32), axis=0)
    grad_second = jnp.einsum(
        "rh,kh->rk", grad_hidden, up_weight, preferred_element_type=jnp.float32
    )
    unused, second_pull = jax.vjp(modulate, middle, shift_two, scale_two)
    grad_middle, grad_shift_two, grad_scale_two = second_pull(grad_second)
    grad_middle = grad_middle + grad_out
    grad_gate_one = grad_middle * branch
    grad_branch = (gate_one * grad_middle).astype(jnp.bfloat16)
    grad_out_weight = jnp.einsum(
        "rk,rd->kd", mixed_rows, grad_branch, preferred_element_type=jnp.float32
    )
    grad_out_bias = jnp.sum(grad_branch.astype(jnp.float32), axis=0)
    grad_mixed = jnp.einsum(
        "rd,kd->rk", grad_branch, out_weight, preferred_element_type=jnp.float32
    ).astype(jnp.bfloat16)
    grad_heads = to_heads(grad_mixed).astype(jnp.float32)
    carried = (grad_heads / totals[:, None, :]).astype(jnp.bfloat16)
    row_delta = jnp.sum(grad_heads * attended_heads, axis=1) / totals
    grad_queries = from_heads(
        query_grads(query_heads, carried, row_delta, query_seg, key_heads, value_heads, seg_all)
    ).astype(jnp.bfloat16)
    delta_all = lax.all_gather(row_delta, "blk", axis=1, tiled=True)
    grad_keys, grad_values = key_grads(
        key_heads, value_heads, query_seg, query_heads, carried, seg_all, delta_all
    )
    grad_joined = jnp.concatenate(
        [
            grad_queries,
            from_heads(grad_keys).astype(jnp.bfloat16),
            from_heads(grad_values).astype(jnp.bfloat16),
        ],
        axis=1,
    )
    grad_qkv = jnp.einsum("rk,rj->kj", first_in, grad_joined, preferred_element_type=jnp.float32)
    grad_qv_bias = jnp.concatenate(
        [
            jnp.sum(grad_queries.astype(jnp.float32), axis=0),
            jnp.sum(grad_joined[:, 2 * features :].astype(jnp.float32), axis=0),
        ]
    )
    grad_first = jnp.einsum(
        "rj,kj->rk", grad_joined, qkv_weight, preferred_element_type=jnp.float32
    )
    unused, first_pull = jax.vjp(modulate, residual, shift_one, scale_one)
    grad_residual, grad_shift_one, grad_scale_one = first_pull(grad_first)
    grad_residual = grad_residual + grad_middle
    grad_per_token = jnp.concatenate(
        [
            grad_shift_one,
            grad_scale_one,
            grad_gate_one,
            grad_shift_two,
            grad_scale_two,
            grad_gate_two,
        ],
        axis=1,
    )
    grad_mod = jnp.einsum("ri,rm->im", onehot, grad_per_token, precision=highest)
    grad_ada_bias = jnp.sum(grad_mod, axis=0)
    local_cond = lax.dynamic_slice_in_dim(silu_cond, image_start, image_count, 0)
    grad_ada = jnp.dot(local_cond.astype(jnp.float32).T, grad_mod, precision=highest)
    pieces = (
        lax.psum_scatter(
            grad_ada.astype(jnp.bfloat16), "dp", scatter_dimension=0, tiled=True
        ).astype(jnp.float32),
        lax.psum_scatter(
            grad_ada_bias.astype(jnp.bfloat16), "dp", scatter_dimension=0, tiled=True
        ).astype(jnp.float32),
        lax.psum_scatter(
            grad_qkv.astype(jnp.bfloat16), "dp", scatter_dimension=0, tiled=True
        ).astype(jnp.float32),
        lax.psum_scatter(
            grad_qv_bias.astype(jnp.bfloat16), "dp", scatter_dimension=0, tiled=True
        ).astype(jnp.float32),
        lax.psum_scatter(
            grad_out_weight.astype(jnp.bfloat16), "dp", scatter_dimension=0, tiled=True
        ).astype(jnp.float32),
        lax.psum_scatter(
            grad_out_bias.astype(jnp.bfloat16), "dp", scatter_dimension=0, tiled=True
        ).astype(jnp.float32),
        lax.psum_scatter(
            grad_up.astype(jnp.bfloat16), "dp", scatter_dimension=0, tiled=True
        ).astype(jnp.float32),
        lax.psum_scatter(
            grad_up_bias.astype(jnp.bfloat16), "dp", scatter_dimension=0, tiled=True
        ).astype(jnp.float32),
        lax.psum_scatter(
            grad_down.astype(jnp.bfloat16), "dp", scatter_dimension=0, tiled=True
        ).astype(jnp.float32),
        lax.psum_scatter(
            grad_down_bias.astype(jnp.bfloat16), "dp", scatter_dimension=0, tiled=True
        ).astype(jnp.float32),
    )
    grads = tuple(
        jax.tree.map(lambda part: part.astype(jnp.float32), lax.psum(as_sent(tuple(pieces)), "blk"))
    )
    return (grad_residual, grads)


def per_device(
    tokens,
    cond,
    segments,
    kept,
    cotangent,
    ada_weight,
    ada_bias,
    qkv_weight,
    qv_bias,
    out_weight,
    out_bias,
    up_weight,
    up_bias,
    down_weight,
    down_bias,
):
    params = (
        ada_weight,
        ada_bias,
        qkv_weight,
        qv_bias,
        out_weight,
        out_bias,
        up_weight,
        up_bias,
        down_weight,
        down_bias,
    )
    image_count = cond.shape[0] // lax.axis_size("dp")
    image_start = lax.axis_index("dp") * image_count
    shard_start = lax.axis_index("dp") * ada_weight.shape[1]
    silu_cond = jax.nn.silu(cond.astype(jnp.float32)).astype(jnp.bfloat16)
    placing = (silu_cond, image_start, image_count, shard_start)
    kept_seg = segments[kept]
    seg_all, kept_seg_all = (
        lax.all_gather(segments, "blk", axis=0, tiled=True),
        lax.all_gather(kept_seg, "blk", axis=0, tiled=True),
    )
    residual = tokens.astype(jnp.float32)
    first_weights = fetch_block(0, params)
    mid, stored_first = forward_block(
        first_weights, residual, segments - image_start, placing, segments, seg_all
    )
    second_weights = fetch_block(1, params)
    routed, stored_second = forward_block(
        second_weights, mid[kept], kept_seg - image_start, placing, kept_seg, kept_seg_all
    )
    final = mid.at[kept].set(routed)
    grad_final = cotangent.astype(jnp.float32)
    grad_routed, grads_second = backward_block(
        second_weights, stored_second, grad_final[kept], placing, kept_seg, kept_seg_all
    )
    grad_mid = grad_final.at[kept].set(grad_routed)
    grad_tokens, grads_first = backward_block(
        first_weights, stored_first, grad_mid, placing, segments, seg_all
    )
    stacked = tuple(
        (
            jnp.stack([first_grad, second_grad])
            for first_grad, second_grad in zip(grads_first, grads_second)
        )
    )
    return (mid, final, grad_tokens) + stacked


def solution(mesh):
    return jax.shard_map(
        per_device,
        mesh=mesh,
        in_specs=(
            P(("dp", "blk"), None),
            P(),
            P(("dp", "blk")),
            P(("dp", "blk")),
            P(("dp", "blk"), None),
            P(None, "dp", None),
            P(None, "dp"),
            P(None, "dp", None),
            P(None, "dp"),
            P(None, "dp", None),
            P(None, "dp"),
            P(None, "dp", None),
            P(None, "dp"),
            P(None, "dp", None),
            P(None, "dp"),
        ),
        out_specs=(
            P(("dp", "blk"), None),
            P(("dp", "blk"), None),
            P(("dp", "blk"), None),
            P(None, "dp", None),
            P(None, "dp"),
            P(None, "dp", None),
            P(None, "dp"),
            P(None, "dp", None),
            P(None, "dp"),
            P(None, "dp", None),
            P(None, "dp"),
            P(None, "dp", None),
            P(None, "dp"),
        ),
        check_vma=False,
    )
```

profile of v0, /device:TPU:0, one launch (start us, length us, event | category | flops | bytes accessed | tf_op | source)
XLA Modules:
  0.0 4082.4 jit_solution(18261401254356577635)
XLA Ops:
  23.0 35.7 all-reduce.21
  59.3 231.0 %all-gather.58.cloned.1.call-done = bf16[1,1152,6912]{2,1,0:T(8,128)(2,1)} async-done(((bf16[1,288,6912]{2,1,0:T(8,128)(2,1)}), bf16[1,1152,6912]{2,1,0:T(8,128)(2,1)}) %all-gather.58.cloned.1.call-update) | async-done | bytes 15925264 | tf_op jit(solution)/shard_map/all_gather | solution.py:166
  290.2 7.7 fusion.159
  304.3 129.2 %all-gather.60.cloned.1.call-done = bf16[1,1152,3456]{2,1,0:T(8,128)(2,1)} async-done(((bf16[1,288,3456]{2,1,0:T(8,128)(2,1)}), bf16[1,1152,3456]{2,1,0:T(8,128)(2,1)}) %all-gather.60.cloned.1.call-update) | async-done | bytes 7962640 | tf_op jit(solution)/shard_map/all_gather | solution.py:168
  458.6 8.9 all-gather.21
  468.7 24.4 all-gather.7
  498.5 208.5 %all-gather.68.cloned.1.call-done = bf16[1,1152,6912]{2,1,0:T(8,128)(2,1)} async-done(((bf16[1,288,6912]{2,1,0:T(8,128)(2,1)}), bf16[1,1152,6912]{2,1,0:T(8,128)(2,1)}) %all-gather.68.cloned.1.call-update) | async-done | bytes 15925264 | tf_op jit(solution)/shard_map/all_gather | solution.py:166
  707.0 7.7 fusion.162
  716.3 30.4 all-gather.44.cloned.1.call-done
  751.5 36.8 all-gather.42.cloned.1.call-done
  793.1 95.8 %while.74 = (s32[]{:T(128)}, f32[16,256]{1,0:T(8,128)}, f32[16,72,256]{2,1,0:T(8,128)}, s32[256]{0:T(256)S(1)}, s32[8,256]{1,0:T(8,128)}, /*index=5*/bf16[8,16,7...) while((s32[]{:T(128)}, f32[16,256]{1,0:T(8,128)}, ...), condition=%wide.region_4.5_spmd.clone, body=%wide.region_2.4_spmd.clone.sunk | while | flops 311037952 | bytes 13112492 | solution.py:69
  900.1 132.6 %all-gather.64.cloned.1.call-done = bf16[1,1152,4608]{2,1,0:T(8,128)(2,1)} async-done(((bf16[1,288,4608]{2,1,0:T(8,128)(2,1)}), bf16[1,1152,4608]{2,1,0:T(8,128)(2,1)}) %all-gather.64.cloned.1.call-update) | async-done | bytes 10616848 | tf_op jit(solution)/shard_map/all_gather | solution.py:172
  1032.6 9.8 fusion.165
  1042.4 176.7 %all-gather.66.cloned.1.call-done = bf16[1,4608,1152]{2,1,0:T(8,128)(2,1)} async-done(((bf16[1,1152,1152]{2,1,0:T(8,128)(2,1)}), bf16[1,4608,1152]{2,1,0:T(8,128)(2,1)}) %all-gather.66.cloned.1.call-update) | async-done | bytes 10616848 | tf_op jit(solution)/shard_map/all_gather | solution.py:174
  1219.1 10.9 multiply_add_fusion
  1239.0 122.5 %all-gather.70.cloned.1.call-done = bf16[1,1152,3456]{2,1,0:T(8,128)(2,1)} async-done(((bf16[1,288,3456]{2,1,0:T(8,128)(2,1)}), bf16[1,1152,3456]{2,1,0:T(8,128)(2,1)}) %all-gather.70.cloned.1.call-update) | async-done | bytes 7962640 | tf_op jit(solution)/shard_map/all_gather | solution.py:168
  1371.6 8.7 all-gather.22
  1380.3 13.1 all-gather.18
  1400.5 25.8 all-gather.46.cloned.1.call-done
  1429.9 24.2 while.75
  1454.2 29.0 all-gather.72.cloned.1.call-done
  1488.2 181.4 %all-gather.74.cloned.1.call-done = bf16[1,1152,4608]{2,1,0:T(8,128)(2,1)} async-done(((bf16[1,288,4608]{2,1,0:T(8,128)(2,1)}), bf16[1,1152,4608]{2,1,0:T(8,128)(2,1)}) %all-gather.74.cloned.1.call-update) | async-done | bytes 10616848 | tf_op jit(solution)/shard_map/all_gather | solution.py:172
  1669.6 7.1 fusion.168
  1676.7 179.1 %all-gather.76.cloned.1.call-done = bf16[1,4608,1152]{2,1,0:T(8,128)(2,1)} async-done(((bf16[1,1152,1152]{2,1,0:T(8,128)(2,1)}), bf16[1,4608,1152]{2,1,0:T(8,128)(2,1)}) %all-gather.76.cloned.1.call-update) | async-done | bytes 10616848 | tf_op jit(solution)/shard_map/all_gather | solution.py:174
  1855.8 10.4 fusion.293
  1877.9 9.2 all_gather.128
  1887.1 34.4 while.76
  1932.8 52.2 %while.77 = (s32[]{:T(128)}, f32[16,72,128]{2,1,0:T(8,128)S(1)}, f32[16,72,128]{2,1,0:T(8,128)}, bf16[8,16,72,128]{3,2,1,0:T(8,128)(2,1)}, s32[8,128]{1,0:T(8,12...) while((s32[]{:T(128)}, f32[16,72,128]{2,1,0:T(8,128)S(1)}, ...), condition=%wide.region_21.22_spmd.clone, body=%wide.region_20.21_spmd.clone.sunk | while | flops 153698304 | bytes 7336072 | solution.py:138
  2002.0 9.6 fusion.294
  2011.6 8.6 multiply_reduce_fusion.1
  2060.1 10.6 convolution_convert_fusion.3
  2079.5 8.4 all_gather.131
  2095.0 84.4 %while.78 = (s32[]{:T(128)}, f32[16,72,256]{2,1,0:T(8,128)}, bf16[8,16,72,256]{3,2,1,0:T(8,128)(2,1)}, s32[256]{0:T(256)S(1)}, s32[8,256]{1,0:T(8,128)}, /*index...) while((s32[]{:T(128)}, f32[16,72,256]{2,1,0:T(8,128)}, ...), condition=%wide.region_29.30_spmd.clone, body=%wide.region_28.29_spmd.clone.sunk | while | flops 460980224 | bytes 13850235 | solution.py:99
  2187.4 113.3 %while.79 = (s32[]{:T(128)}, f32[16,72,256]{2,1,0:T(8,128)}, f32[16,72,256]{2,1,0:T(8,128)S(1)}, bf16[8,16,72,256]{3,2,1,0:T(8,128)(2,1)}, s32[8,256]{1,0:T(8,12...) while((s32[]{:T(128)}, f32[16,72,256]{2,1,0:T(8,128)}, ...), condition=%wide.region_31.32_spmd.clone, body=%wide.region_30.31_spmd.clone.sunk | while | flops 616759296 | bytes 21125256 | solution.py:138
  2317.6 7.1 multiply_dynamic-update-slice_fusion.3
  2328.1 15.5 convolution_convert_fusion
  2360.2 15.5 convolution_convert_fusion.1
  2375.9 127.8 %reduce-scatter.25.cloned.1.call-done = bf16[288,4608]{1,0:T(8,128)(2,1)} async-done(((bf16[1152,4608]{1,0:T(8,128)(2,1)}), bf16[288,4608]{1,0:T(8,128)(2,1)}) %reduce-scatter.25.cloned.1.call-update) | async-done | bytes 2654224 | tf_op jit(solution)/shard_map/reduce_scatter | solution.py:366
  2503.7 183.5 %reduce-scatter.29.cloned.1.call-done = bf16[1152,1152]{1,0:T(8,128)(2,1)} async-done(((bf16[4608,1152]{1,0:T(8,128)(2,1)}), bf16[1152,1152]{1,0:T(8,128)(2,1)}) %reduce-scatter.29.cloned.1.call-update) | async-done | bytes 2654224 | tf_op jit(solution)/shard_map/reduce_scatter | solution.py:372
  2687.2 183.6 %reduce-scatter.27.cloned.1.call-done = bf16[1152,1152]{1,0:T(8,128)(2,1)} async-done(((bf16[4608,1152]{1,0:T(8,128)(2,1)}), bf16[1152,1152]{1,0:T(8,128)(2,1)}) %reduce-scatter.27.cloned.1.call-update) | async-done | bytes 2654224 | tf_op jit(solution)/shard_map/reduce_scatter | solution.py:372
  2870.7 184.1 %reduce-scatter.23.cloned.1.call-done = bf16[288,4608]{1,0:T(8,128)(2,1)} async-done(((bf16[1152,4608]{1,0:T(8,128)(2,1)}), bf16[288,4608]{1,0:T(8,128)(2,1)}) %reduce-scatter.23.cloned.1.call-update) | async-done | bytes 2654224 | tf_op jit(solution)/shard_map/reduce_scatter | solution.py:366
  3054.8 141.5 %reduce-scatter.15.cloned.1.call-done = bf16[288,3456]{1,0:T(8,128)(2,1)} async-done(((bf16[1152,3456]{1,0:T(8,128)(2,1)}), bf16[288,3456]{1,0:T(8,128)(2,1)}) %reduce-scatter.15.cloned.1.call-update) | async-done | bytes 1990672 | tf_op jit(solution)/shard_map/reduce_scatter | solution.py:354
  3196.3 270.8 %reduce-scatter.13.cloned.1.call-done = bf16[288,6912]{1,0:T(8,128)(2,1)} async-done(((bf16[1152,6912]{1,0:T(8,128)(2,1)}), bf16[288,6912]{1,0:T(8,128)(2,1)}) %reduce-scatter.13.cloned.1.call-update) | async-done | bytes 3981328 | tf_op jit(solution)/shard_map/reduce_scatter | solution.py:348
  3467.2 270.5 %reduce-scatter.11.cloned.1.call-done = bf16[288,6912]{1,0:T(8,128)(2,1)} async-done(((bf16[1152,6912]{1,0:T(8,128)(2,1)}), bf16[288,6912]{1,0:T(8,128)(2,1)}) %reduce-scatter.11.cloned.1.call-update) | async-done | bytes 3981328 | tf_op jit(solution)/shard_map/reduce_scatter | solution.py:348
  3744.9 19.4 all-reduce.20
  3765.2 24.8 all-reduce.18
  3793.0 253.9 %all-reduce.24.cloned.1.call-done = (bf16[1,288,6912]{2,1,0:T(8,128)(2,1)}, bf16[1,288,6912]{2,1,0:T(8,128)(2,1)}, bf16[1,288,3456]{2,1,0:T(8,128)(2,1)}, bf16[1...) async-done(((bf16[1,288,6912]{2,1,0:T(8,128)(2,1)}, ...) | async-done | bytes 23887888 | tf_op jit(solution)/shard_map/psum | solution.py:380
  4047.0 7.5 maximum_convert_fusion.2
  (818 shorter events, 679.4 us)
Async XLA Ops:
  7.2 283.0 %all-gather.58.cloned.1.call-start = ((), (), s32[]{:S(2)}) async-start(), calls=%async_computation.28 | async-start | bytes 19906560 | tf_op jit(solution)/shard_map/all_gather | solution.py:166
  12.9 420.6 %all-gather.60.cloned.1.call-start = ((), (), s32[]{:S(2)}) async-start(), calls=%async_computation.29 | async-start | bytes 9953280 | tf_op jit(solution)/shard_map/all_gather | solution.py:168
  17.4 689.6 %all-gather.68.cloned.1.call-start = ((), (), s32[]{:S(2)}) async-start(), calls=%async_computation.33 | async-start | bytes 19906560 | tf_op jit(solution)/shard_map/all_gather | solution.py:166
  17.4 41.7 %copy-start = (s32[256]{0:T(256)S(1)}, s32[256]{0:T(256)}, u32[]{:S(2)}) copy-start(s32[256]{0:T(256)} %param.29) | copy-start | bytes 3076
  18.1 728.6 %all-gather.44.cloned.1.call-start = ((), (), s32[]{:S(2)}) async-start(), calls=%async_computation.11 | async-start | bytes 5308416 | tf_op jit(solution)/shard_map/all_gather | solution.py:56
  58.6 648.4 %copy-start.75 = (f32[20,1152]{1,0:T(8,128)}, f32[20,1152]{1,0:T(8,128)S(1)}, u32[]{:S(2)}) copy-start(f32[20,1152]{1,0:T(8,128)S(1)} %convert_element_type.367) | copy-start | bytes 276484
  58.9 242.0 %copy-start.96 = (f32[256]{0:T(256)}, f32[256]{0:T(256)S(1)}, u32[]{:S(2)}) copy-start(f32[256]{0:T(256)S(1)} %broadcast_multiply_fusion.1) | copy-start | bytes 3076
  59.2 238.7 %copy-start.114 = (f32[256]{0:T(256)}, f32[256]{0:T(256)S(1)}, u32[]{:S(2)}) copy-start(f32[256]{0:T(256)S(1)} %fusion.226) | copy-start | bytes 3076
  59.2 238.7 %copy-start.86 = (s32[256]{0:T(256)}, s32[256]{0:T(256)S(1)}, u32[]{:S(2)}) copy-start(s32[256]{0:T(256)S(1)} %broadcast_subtract_fusion) | copy-start | bytes 3076
  59.2 241.7 %copy-start.112 = (f32[256]{0:T(256)}, f32[256]{0:T(256)S(1)}, u32[]{:S(2)}) copy-start(f32[256]{0:T(256)S(1)} %fusion.261) | copy-start | bytes 3076
  304.3 135.1 %copy-start.42 = (bf16[256,1152]{1,0:T(8,128)(2,1)}, bf16[256,1152]{1,0:T(8,128)(2,1)S(1)}, u32[]{:S(2)}) copy-start(bf16[256,1152]{1,0:T(8,128)(2,1)S(1)} %fusion.224) | copy-start | bytes 1769476
  442.4 345.8 %all-gather.42.cloned.1.call-start = ((), (), s32[]{:S(2)}) async-start(), calls=%async_computation.10 | async-start | bytes 5308416 | tf_op jit(solution)/shard_map/all_gather | solution.py:55
  445.1 446.0 %all-gather.62.cloned.1.call-start = ((), (), s32[]{:S(2)}) async-start(), calls=%async_computation.30 | async-start | bytes 3317760 | tf_op jit(solution)/shard_map/all_gather | solution.py:170
  446.4 586.3 %all-gather.64.cloned.1.call-start = ((), (), s32[]{:S(2)}) async-start(), calls=%async_computation.31 | async-start | bytes 13271040 | tf_op jit(solution)/shard_map/all_gather | solution.py:172
  452.2 766.9 %all-gather.66.cloned.1.call-start = ((), (), s32[]{:S(2)}) async-start(), calls=%async_computation.32 | async-start | bytes 13271040 | tf_op jit(solution)/shard_map/all_gather | solution.py:174
  457.7 903.8 %all-gather.70.cloned.1.call-start = ((), (), s32[]{:S(2)}) async-start(), calls=%async_computation.34 | async-start | bytes 9953280 | tf_op jit(solution)/shard_map/all_gather | solution.py:168
  458.5 938.5 %all-gather.48.cloned.1.call-start = ((), (), s32[]{:S(2)}) async-start(), calls=%async_computation.13 | async-start | bytes 2654208 | tf_op jit(solution)/shard_map/all_gather | solution.py:56
  494.9 212.1 %copy-start.121 = (s32[1024]{0:T(1024)}, s32[1024]{0:T(1024)S(1)}, u32[]{:S(2)}) copy-start(s32[1024]{0:T(1024)S(1)} %pad_clamp_fusion) | copy-start | bytes 12292
  716.3 520.1 %copy-start.6 = (f32[128,6912]{1,0:T(8,128)}, f32[128,6912]{1,0:T(8,128)S(1)}, u32[]{:S(2)}) copy-start(f32[128,6912]{1,0:T(8,128)S(1)} %fusion.252) | copy-start | bytes 10616836
  900.1 319.0 %copy-start.120 = (f32[1152]{0:T(1024)S(1)}, f32[1152]{0:T(1024)}, u32[]{:S(2)}) copy-start(f32[1152]{0:T(1024)} %convert_element_type.466) | copy-start | bytes 13828
  1239.0 127.3 %copy-start.88 = (f32[1152]{0:T(1024)S(1)}, f32[1152]{0:T(1024)}, u32[]{:S(2)}) copy-start(f32[1152]{0:T(1024)} %get-tuple-element.529) | copy-start | bytes 13828
  1239.0 127.3 %copy-start.89 = (f32[1152]{0:T(1024)S(1)}, f32[1152]{0:T(1024)}, u32[]{:S(2)}) copy-start(f32[1152]{0:T(1024)} %get-tuple-element.530) | copy-start | bytes 13828
  1367.3 59.0 %all-gather.46.cloned.1.call-start = ((), (), s32[]{:S(2)}) async-start(), calls=%async_computation.12 | async-start | bytes 2654208 | tf_op jit(solution)/shard_map/all_gather | solution.py:55
  1368.3 114.8 %all-gather.72.cloned.1.call-start = ((), (), s32[]{:S(2)}) async-start(), calls=%async_computation.35 | async-start | bytes 3317760 | tf_op jit(solution)/shard_map/all_gather | solution.py:170
  1368.9 300.6 %all-gather.74.cloned.1.call-start = ((), (), s32[]{:S(2)}) async-start(), calls=%async_computation.36 | async-start | bytes 13271040 | tf_op jit(solution)/shard_map/all_gather | solution.py:172
  1369.7 486.2 %all-gather.76.cloned.1.call-start = ((), (), s32[]{:S(2)}) async-start(), calls=%async_computation.37 | async-start | bytes 13271040 | tf_op jit(solution)/shard_map/all_gather | solution.py:174
  1370.3 553.9 %all-gather.50.cloned.1.call-start = ((), (), s32[]{:S(2)}) async-start(), calls=%async_computation.14 | async-start | bytes 2654208 | tf_op jit(solution)/shard_map/all_gather | solution.py:115
  1396.9 531.7 %all-gather.52.cloned.1.call-start = ((), (), s32[]{:S(2)}) async-start(), calls=%async_computation.15 | async-start | bytes 2654208 | tf_op jit(solution)/shard_map/all_gather | solution.py:116
  1429.9 53.3 %copy-start.12 = (f32[128,1152]{1,0:T(8,128)S(1)}, f32[128,1152]{1,0:T(8,128)}, u32[]{:S(2)}) copy-start(f32[128,1152]{1,0:T(8,128)} %gather_fusion) | copy-start | bytes 1769476
  1486.5 384.7 %copy-start.14 = (f32[128,1152]{1,0:T(8,128)}, f32[128,1152]{1,0:T(8,128)S(1)}, u32[]{:S(2)}) copy-start(f32[128,1152]{1,0:T(8,128)S(1)} %get-tuple-element.714) | copy-start | bytes 1769476
  1486.5 384.7 %copy-start.107 = (f32[128]{0:T(128)}, f32[128]{0:T(128)S(1)}, u32[]{:S(2)}) copy-start(f32[128]{0:T(128)S(1)} %broadcast_multiply_fusion.2) | copy-start | bytes 1540
  1486.7 384.5 %copy-start.124 = (f32[128]{0:T(128)}, f32[128]{0:T(128)S(1)}, u32[]{:S(2)}) copy-start(f32[128]{0:T(128)S(1)} %fusion.264) | copy-start | bytes 1540
  1488.2 188.5 %copy-start.40 = (bf16[128,1152]{1,0:T(8,128)(2,1)}, bf16[128,1152]{1,0:T(8,128)(2,1)S(1)}, u32[]{:S(2)}) copy-start(bf16[128,1152]{1,0:T(8,128)(2,1)S(1)} %fusion.233) | copy-start | bytes 884740
  1877.2 193.6 %all-gather.54.cloned.1.call-start = ((), (), s32[]{:S(2)}) async-start(), calls=%async_computation.16 | async-start | bytes 5308416 | tf_op jit(solution)/shard_map/all_gather | solution.py:115
  1877.8 301.6 %all-gather.56.cloned.1.call-start = ((), (), s32[]{:S(2)}) async-start(), calls=%async_computation.17 | async-start | bytes 5308416 | tf_op jit(solution)/shard_map/all_gather | solution.py:116
  1932.8 54.4 %copy-start.119 = (f32[128]{0:T(128)S(1)}, f32[128]{0:T(128)}, u32[]{:S(2)}) copy-start(f32[128]{0:T(128)} %copy-done.118) | copy-start | bytes 1540
  2032.1 343.7 %reduce-scatter.21.cloned.1.call-start = ((), (), s32[]{:S(2)}) async-start(), calls=%async_computation.23 | async-start | bytes 3317760 | tf_op jit(solution)/shard_map/reduce_scatter | solution.py:360
  2034.6 341.3 %reduce-scatter.19.cloned.1.call-start = ((), (), s32[]{:S(2)}) async-start(), calls=%async_computation.22 | async-start | bytes 3317760 | tf_op jit(solution)/shard_map/reduce_scatter | solution.py:360
  2037.2 338.7 %reduce-scatter.17.cloned.1.call-start = ((), (), s32[]{:S(2)}) async-start(), calls=%async_computation.21 | async-start | bytes 9953280 | tf_op jit(solution)/shard_map/reduce_scatter | solution.py:354
  2043.9 459.8 %reduce-scatter.25.cloned.1.call-start = ((), (), s32[]{:S(2)}) async-start(), calls=%async_computation.25 | async-start | bytes 13271040 | tf_op jit(solution)/shard_map/reduce_scatter | solution.py:366
  2050.9 636.3 %reduce-scatter.29.cloned.1.call-start = ((), (), s32[]{:S(2)}) async-start(), calls=%async_computation.27 | async-start | bytes 13271040 | tf_op jit(solution)/shard_map/reduce_scatter | solution.py:372
  2059.0 811.7 %reduce-scatter.27.cloned.1.call-start = ((), (), s32[]{:S(2)}) async-start(), calls=%async_computation.26 | async-start | bytes 13271040 | tf_op jit(solution)/shard_map/reduce_scatter | solution.py:372
  2070.7 984.1 %reduce-scatter.23.cloned.1.call-start = ((), (), s32[]{:S(2)}) async-start(), calls=%async_computation.24 | async-start | bytes 13271040 | tf_op jit(solution)/shard_map/reduce_scatter | solution.py:366
  2093.7 1102.6 %reduce-scatter.15.cloned.1.call-start = ((), (), s32[]{:S(2)}) async-start(), calls=%async_computation.20 | async-start | bytes 9953280 | tf_op jit(solution)/shard_map/reduce_scatter | solution.py:354
  2312.3 1154.9 %reduce-scatter.13.cloned.1.call-start = ((), (), s32[]{:S(2)}) async-start(), calls=%async_computation.19 | async-start | bytes 19906560 | tf_op jit(solution)/shard_map/reduce_scatter | solution.py:348
  2343.7 1394.0 %reduce-scatter.11.cloned.1.call-start = ((), (), s32[]{:S(2)}) async-start(), calls=%async_computation.18 | async-start | bytes 19906560 | tf_op jit(solution)/shard_map/reduce_scatter | solution.py:348
  2375.8 1671.2 %all-reduce.24.cloned.1.call-start = ((), (), s32[]{:S(2)}) async-start(), calls=%async_computation.38 | async-start | bytes 47775744 | tf_op jit(solution)/shard_map/psum | solution.py:380
  3744.6 309.9 %copy-start.70 = (f32[256,1152]{1,0:T(8,128)}, f32[256,1152]{1,0:T(8,128)S(1)}, u32[]{:S(2)}) copy-start(f32[256,1152]{1,0:T(8,128)S(1)} %scatter_custom_fusion) | copy-start | bytes 3538948
  (133 other events, 703.3 us)
Sparse Core Ops, SparseCore 0:
  13.0 277.1 all-gather.57
  292.4 141.1 all-gather.59
  435.7 271.3 all-gather.67
  708.7 37.9 all-gather.43
  748.5 39.7 all-gather.41
  790.3 55.3 all-gather.61
  847.8 184.8 all-gather.63
  1034.8 184.2 all-gather.65
  1220.7 140.8 all-gather.69
  1367.5 27.5 all-gather.47
  1396.9 29.3 all-gather.45
  1427.7 55.3 all-gather.71
  1484.7 184.8 all-gather.73
  1671.6 184.2 all-gather.75
  1857.6 27.6 all-gather.49
  1887.0 29.3 all-gather.51
  1918.2 39.7 all-gather.53
  2032.2 36.7 all-gather.55
  2071.9 52.6 reduce-scatter.20
  2126.8 52.2 reduce-scatter.18
  2182.0 137.7 reduce-scatter.16
  2322.9 180.6 reduce-scatter.24
  2506.0 181.1 reduce-scatter.28
  2689.5 181.1 reduce-scatter.26
  2873.7 181.1 reduce-scatter.22
  3057.2 139.1 reduce-scatter.14
  3199.1 267.9 reduce-scatter.12
  3469.7 268.0 reduce-scatter.10
  3743.6 303.2 all-reduce.23
where the time goes:
time: 4090 us; the launch traced here: 4080 us
  waiting for transfers between devices  3100 us (76%)
  matrix products  568 us (14%)
  blocking collectives  153 us (4%)
  local copies, waits for them, and re-layouts  137 us (3%)
  other arithmetic  97.7 us (2%)
    reduce_scatter x2, waiting for transfers between devices, backward_block(): lax.psum_scatter(grad_ada.astype(jnp.bfloat16), 'dp', scatter_dimension=0...  541 us
    all_gather x2, waiting for transfers between devices, fetch_block(): lax.all_gather(ada_weight[layer_index], 'dp', axis=0, tiled=True)  439 us
    reduce_scatter x2, waiting for transfers between devices, backward_block(): lax.psum_scatter(grad_down.astype(jnp.bfloat16), 'dp', scatter_dimension=...  367 us
    all_gather x2, waiting for transfers between devices, fetch_block(): lax.all_gather(down_weight[layer_index], 'dp', axis=0, tiled=True)  356 us
    all_gather x2, waiting for transfers between devices, fetch_block(): lax.all_gather(up_weight[layer_index], 'dp', axis=0, tiled=True)  314 us
    reduce_scatter x2, waiting for transfers between devices, backward_block(): lax.psum_scatter(grad_up.astype(jnp.bfloat16), 'dp', scatter_dimension=0,...  312 us
    psum x1, waiting for transfers between devices, backward_block(): lax.psum(as_sent(tuple(pieces)), 'blk')  254 us
    all_gather x2, waiting for transfers between devices, fetch_block(): lax.all_gather(qkv_weight[layer_index], 'dp', axis=0, tiled=True)  252 us
  transfers between devices with their start and end apart: 29, of which 20 were waited for; matrix products, arithmetic and copies ran while one was open for 18% of the time, Pallas kernels for 0%

commit v1 on v0

v1 whole, which is shorter than its diff:
```python
import functools
import math

import jax
import jax.numpy as jnp
from jax import lax
from jax.experimental import pallas as pl
from jax.experimental.pallas import tpu as pltpu
from jax.sharding import PartitionSpec as P

HEADS = 16
BIG_LEN = 1024
SMALL_LEN = 256
PAD = 128
epsilon = 1e-06
highest = lax.Precision.HIGHEST
bf16 = jnp.bfloat16
f32 = jnp.float32
VMEM_LIMIT = 56 * 1024 * 1024

NN = (((1,), (0,)), ((), ()))
NT = (((1,), (1,)), ((), ()))
TN = (((0,), (0,)), ((), ()))


def dot(left, right, dims=NN):
    return lax.dot_general(left, right, dims, preferred_element_type=f32)


def swap(x, bit, n):
    return lax.ppermute(x, "blk", [(i, i ^ bit) for i in range(n)])


def gather_rows(x, n):
    if n == 8:
        rows = x.shape[0]
        half = rows // 2
        c1 = swap(x, 1, n)
        x2 = swap(x, 2, n)
        x4 = swap(x, 4, n)
        d0 = swap(x4[:half], 2, n)
        d1 = swap(x2[half:], 4, n)
        x3 = swap(x2, 1, n)
        x5 = swap(x4, 1, n)
        e0 = swap(d0, 1, n)
        e1 = swap(d1, 1, n)
        return [
            (x, 0, 0),
            (c1, 1, 0),
            (x2, 2, 0),
            (x3, 3, 0),
            (x4, 4, 0),
            (x5, 5, 0),
            (d0, 6, 0),
            (d1, 6, half),
            (e0, 7, 0),
            (e1, 7, half),
        ]
    pieces = {0: x}
    bit = n // 2
    while bit:
        for k in list(pieces):
            pieces[k | bit] = swap(pieces[k], bit, n)
        bit //= 2
    return [(pieces[k], k, 0) for k in sorted(pieces)]


def reduce_rows(even, odd, n):
    got = swap(odd, 1, n)
    total = even.astype(f32) + got.astype(f32)
    if n == 8:
        half = total.shape[1] // 2
        q0, q1, q2, q3 = (total[j] for j in range(4))
        s3 = q3.astype(bf16)
        a0 = swap(s3[:half], 2, n)
        a1 = swap(s3[half:], 4, n)
        r1a = swap(q1[:half].astype(bf16), 2, n)
        r2b = swap(q2[half:].astype(bf16), 4, n)
        r1b = swap((q1[half:] + a1.astype(f32)).astype(bf16), 2, n)
        r2a = swap((q2[:half] + a0.astype(f32)).astype(bf16), 4, n)
        top = q0[:half] + r1a.astype(f32) + r2a.astype(f32)
        low = q0[half:] + r1b.astype(f32) + r2b.astype(f32)
        return jnp.concatenate([top, low], axis=0)
    bit = n // 2
    while bit > 1:
        step = bit // 2
        got = swap(total[step:].astype(bf16), bit, n)
        total = total[:step] + got.astype(f32)
        bit //= 2
    return total[0]


def load_chunks(chunks, refs, held, sems):
    copies = []
    for i, (k, off, rows) in enumerate(chunks):
        copies.append(pltpu.make_async_copy(refs[i], held.at[k, pl.ds(off, rows)], sems.at[i]))
    for copy in copies:
        copy.start()
    for copy in copies:
        copy.wait()


def chunk_plan(chunks):
    return tuple((k, off, array.shape[0]) for array, k, off in chunks)


def call(kernel, name, chunks, args, outs, scratch, flops):
    arrays = [c[0] for c in chunks]
    moved = sum(a.size * a.dtype.itemsize for a in arrays + list(args))
    moved += sum(math.prod(o.shape) * o.dtype.itemsize for o in outs)
    sems = [pltpu.SemaphoreType.DMA((max(1, len(arrays)),))]
    vmem = pl.BlockSpec(memory_space=pltpu.VMEM)
    return pl.pallas_call(
        kernel,
        name=name,
        out_shape=outs,
        in_specs=[pl.BlockSpec(memory_space=pl.ANY)] * len(arrays) + [vmem] * len(args),
        out_specs=[vmem] * len(outs),
        scratch_shapes=scratch + sems,
        compiler_params=pltpu.CompilerParams(vmem_limit_bytes=VMEM_LIMIT),
        cost_estimate=pl.CostEstimate(flops=flops, bytes_accessed=moved, transcendentals=0),
    )(*arrays, *args)


def sds(shape, dtype):
    return jax.ShapeDtypeStruct(shape, dtype)


def attn_forward_kernel(plan, images, masked, scale, nh, *refs):
    count = len(plan)
    chunk_refs, refs = refs[:count], refs[count:]
    wqkv, bias, wout = refs[:3]
    refs = refs[3:]
    if masked:
        seg_col, seg_row = refs[:2]
        refs = refs[2:]
    qkv, al, mixed, even, odd, held, rowmix, sems = refs
    n, rows, feats = held.shape
    parts = 3 * nh
    hd = wout.shape[0] // nh
    load_chunks(plan, chunk_refs, held, sems)

    @pl.loop(0, n)
    def _(k):
        proj = (dot(held[k], wqkv[...]) + bias[...]).astype(bf16)
        for p in range(parts):
            part = proj[:, p * PAD : (p + 1) * PAD]
            for off, size, base in images:
                qkv[p, pl.ds(base + k * size, size), :] = part[off : off + size]

    lane = lax.broadcasted_iota(jnp.int32, (1, PAD), 1)
    for off, size, base in images:
        length = size * n
        tile = min(256, length)

        @pl.loop(0, nh * (length // tile))
        def _(step):
            h = step // (length // tile)
            start = base + (step % (length // tile)) * tile
            q = qkv[h, pl.ds(start, tile), :]
            keys = qkv[nh + h, pl.ds(base, length), :]
            vals = qkv[2 * nh + h, pl.ds(base, length), :]
            e = jnp.exp2(dot(q, keys, NT) * (scale * math.log2(math.e)))
            if masked:
                e = jnp.where(seg_col[pl.ds(start, tile), :] == seg_row[...], e, 0.0)
            acc = dot(e.astype(bf16), vals)
            l = acc[:, PAD_L : PAD_L + 1]
            attn = acc / l
            al[h, pl.ds(start, tile), :] = jnp.where(lane == PAD_L, l, attn)
            rowmix[h, pl.ds(start, tile), :] = attn.astype(bf16)

    @pl.loop(0, n // 2)
    def _(j):
        for side, out in ((0, even), (1, odd)):
            k = 2 * j + side
            for off, size, base in images:
                for h in range(nh):
                    mixed[k, pl.ds(off, size), h * PAD : (h + 1) * PAD] = rowmix[
                        h, pl.ds(base + k * size, size), :
                    ]
            out[j] = dot(mixed[k], wout[...]).astype(bf16)


PAD_L = 72


def attn_forward(chunks, wqkv, bias, wout, segs, n, images, scale, nh):
    rows = sum(size for _, size, _ in images)
    total = rows * n
    feats = wqkv.shape[0]
    masked = segs is not None
    outs = [
        sds((3 * nh, total, PAD), bf16),
        sds((nh, total, PAD), f32),
        sds((n, rows, nh * PAD), bf16),
        sds((n // 2, rows, feats), bf16),
        sds((n // 2, rows, feats), bf16),
    ]
    scratch = [pltpu.VMEM((n, rows, feats), bf16), pltpu.VMEM((nh, total, PAD), bf16)]
    flops = 2 * total * feats * 4 * nh * PAD + 4 * nh * total * total * PAD
    return call(
        functools.partial(attn_forward_kernel, chunk_plan(chunks), images, masked, scale, nh),
        "attn_forward",
        chunks,
        [wqkv, bias, wout] + (list(segs) if masked else []),
        outs,
        scratch,
        flops,
    )


def attn_backward_kernel(plan, images, masked, scale, nh, *refs):
    count = len(plan)
    chunk_refs, refs = refs[:count], refs[count:]
    wqkv, wout, qkv, al = refs[:4]
    refs = refs[4:]
    if masked:
        seg_col, seg_row = refs[:2]
        refs = refs[2:]
    dqkv, sums, even, odd, held, gext, grads, dqt, sems = refs
    n, rows, feats = held.shape
    parts = 3 * nh
    load_chunks(plan, chunk_refs, held, sems)
    lane = lax.broadcasted_iota(jnp.int32, (1, PAD), 1)

    @pl.loop(0, n)
    def _(k):
        d_all = dot(held[k], wout[...], NT).astype(bf16).astype(f32)
        for h in range(nh):
            d_head = d_all[:, h * PAD : (h + 1) * PAD]
            for off, size, base in images:
                here = pl.ds(base + k * size, size)
                known = al[h, here, :]
                d = d_head[off : off + size]
                inverse = 1.0 / known[:, PAD_L : PAD_L + 1]
                dotted = jnp.where(lane < PAD_L, d * known, 0.0)
                minus = -jnp.sum(dotted, axis=1, keepdims=True) * inverse
                top = minus.astype(bf16).astype(f32)
                ext = jnp.where(lane == PAD_L, top, jnp.where(lane == PAD_L + 1, minus - top, 0.0))
                gext[h, here, :] = jnp.where(lane < PAD_L, d * inverse, ext).astype(bf16)

    for off, size, base in images:
        length = size * n
        tile = min(256, length)

        @pl.loop(0, nh)
        def _(h):
            queries = qkv[h, pl.ds(base, length), :]
            carried = gext[h, pl.ds(base, length), :]

            @pl.loop(0, length // tile)
            def _(t):
                here = pl.ds(base + t * tile, tile)
                keys = qkv[nh + h, here, :]
                vals = qkv[2 * nh + h, here, :]
                e = jnp.exp2(dot(keys, queries, NT) * (scale * math.log2(math.e)))
                if masked:
                    e = jnp.where(seg_col[here, :] == seg_row[...], e, 0.0)
                er = e.astype(bf16)
                raw = (e * dot(vals, carried, NT)).astype(bf16)
                dv = jnp.where(lane < PAD_L, dot(er, carried), 0.0)
                grads[2 * nh + h, here, :] = dv.astype(bf16)
                grads[nh + h, here, :] = (dot(raw, queries) * scale).astype(bf16)
                added = dot(keys.T, raw)

                @pl.when(t == 0)
                def _():
                    dqt[:, :length] = added

                @pl.when(t > 0)
                def _():
                    dqt[:, :length] += added

            grads[h, pl.ds(base, length), :] = (dqt[:, :length].T * scale).astype(bf16)

    sums[...] = jnp.zeros_like(sums)

    @pl.loop(0, n // 2)
    def _(j):
        for side, out in ((0, even), (1, odd)):
            k = 2 * j + side
            for off, size, base in images:
                for p in range(parts):
                    dqkv[k, pl.ds(off, size), p * PAD : (p + 1) * PAD] = grads[
                        p, pl.ds(base + k * size, size), :
                    ]
            block = dqkv[k]
            sums[...] += jnp.sum(block.astype(f32), axis=0, keepdims=True)
            out[j] = dot(block, wqkv[...], NT).astype(bf16)


def attn_backward(chunks, wqkv, wout, qkv, al, segs, n, images, scale, nh):
    rows = sum(size for _, size, _ in images)
    total = rows * n
    feats = wqkv.shape[0]
    masked = segs is not None
    longest = max(size for _, size, _ in images) * n
    outs = [
        sds((n, rows, 3 * nh * PAD), bf16),
        sds((1, 3 * nh * PAD), f32),
        sds((n // 2, rows, feats), bf16),
        sds((n // 2, rows, feats), bf16),
    ]
    scratch = [
        pltpu.VMEM((n, rows, feats), bf16),
        pltpu.VMEM((nh, total, PAD), bf16),
        pltpu.VMEM((3 * nh, total, PAD), bf16),
        pltpu.VMEM((PAD, longest), f32),
    ]
    flops = 2 * total * feats * 4 * nh * PAD + 10 * nh * total * total * PAD
    return call(
        functools.partial(attn_backward_kernel, chunk_plan(chunks), images, masked, scale, nh),
        "attn_backward",
        chunks,
        [wqkv, wout, qkv, al] + (list(segs) if masked else []),
        outs,
        scratch,
        flops,
    )


def attn_weights_kernel(plan_first, plan_back, *refs):
    a, b = len(plan_first), len(plan_back)
    first_refs, back_refs, refs = refs[:a], refs[a : a + b], refs[a + b :]
    dqkv, mixed, spread, g_qkv, g_out, sums, held, wide, sems = refs
    n, rows, feats = held.shape
    load_chunks(plan_first, first_refs, held, sems)
    left = held[...].reshape(n * rows, feats)
    right = dqkv[...].reshape(n * rows, dqkv.shape[2])
    wide[...] = dot(left, right, TN).astype(bf16)
    g_qkv[...] = dot(wide[...], spread[...], NT).astype(bf16)
    load_chunks(plan_back, back_refs, held, sems)
    back = held[...].reshape(n * rows, feats)
    sums[...] = jnp.sum(back.astype(f32), axis=0, keepdims=True)
    left = mixed[...].reshape(n * rows, mixed.shape[2])
    tall = dot(left, back, TN).astype(bf16)
    width, wider = g_out.shape[0], tall.shape[0]
    g_out[...] = dot(spread[:width, :wider], tall).astype(bf16)


def attn_weights(first_chunks, back_chunks, dqkv, mixed, spread, nh, hd):
    n, rows, _ = dqkv.shape
    feats = first_chunks[0][0].shape[1]
    outs = [sds((feats, 3 * nh * hd), bf16), sds((nh * hd, feats), bf16), sds((1, feats), f32)]
    scratch = [
        pltpu.VMEM((n, rows, feats), bf16),
        pltpu.VMEM((feats, dqkv.shape[2]), bf16),
    ]
    return call(
        functools.partial(attn_weights_kernel, chunk_plan(first_chunks), chunk_plan(back_chunks)),
        "attn_weights",
        first_chunks + back_chunks,
        [dqkv, mixed, spread],
        outs,
        scratch,
        2 * n * rows * feats * 4 * nh * PAD,
    )


def gelu_and_slope(u):
    c = math.sqrt(2.0 / math.pi)
    square = u * u
    t = jnp.tanh(c * u * (1.0 + 0.044715 * square))
    half = 0.5 * (1.0 + t)
    slope = half + 0.5 * u * (1.0 - t * t) * (c * (1.0 + 3.0 * 0.044715 * square))
    return u * half, slope


def mlp_forward_kernel(plan, *refs):
    count = len(plan)
    chunk_refs, refs = refs[:count], refs[count:]
    wup, bias, wdown, active, slope, even, odd, held, sems = refs
    n = held.shape[0]
    load_chunks(plan, chunk_refs, held, sems)

    @pl.loop(0, n // 2)
    def _(j):
        for side, out in ((0, even), (1, odd)):
            k = 2 * j + side
            act, slp = gelu_and_slope(dot(held[k], wup[...]) + bias[...])
            act = act.astype(bf16)
            active[k] = act
            slope[k] = slp.astype(bf16)
            out[j] = dot(act, wdown[...]).astype(bf16)


def mlp_forward(chunks, wup, bias, wdown, n):
    rows, feats = chunks[0][0].shape
    hidden = wup.shape[1]
    outs = [
        sds((n, rows, hidden), bf16),
        sds((n, rows, hidden), bf16),
        sds((n // 2, rows, feats), bf16),
        sds((n // 2, rows, feats), bf16),
    ]
    return call(
        functools.partial(mlp_forward_kernel, chunk_plan(chunks)),
        "mlp_forward",
        chunks,
        [wup, bias, wdown],
        outs,
        [pltpu.VMEM((n, rows, feats), bf16)],
        4 * n * rows * feats * hidden,
    )


def mlp_backward_kernel(plan, *refs):
    count = len(plan)
    chunk_refs, refs = refs[:count], refs[count:]
    wup, wdown, slope, back, even, odd, held, sems = refs
    n = held.shape[0]
    load_chunks(plan, chunk_refs, held, sems)

    @pl.loop(0, n // 2)
    def _(j):
        for side, out in ((0, even), (1, odd)):
            k = 2 * j + side
            grad = (dot(held[k], wdown[...], NT) * slope[k].astype(f32)).astype(bf16)
            back[k] = grad
            out[j] = dot(grad, wup[...], NT).astype(bf16)


def mlp_backward(chunks, wup, wdown, slope):
    n, rows, hidden = slope.shape
    feats = wup.shape[0]
    outs = [
        sds((n, rows, hidden), bf16),
        sds((n // 2, rows, feats), bf16),
        sds((n // 2, rows, feats), bf16),
    ]
    return call(
        functools.partial(mlp_backward_kernel, chunk_plan(chunks)),
        "mlp_backward",
        chunks,
        [wup, wdown, slope],
        outs,
        [pltpu.VMEM((n, rows, feats), bf16)],
        4 * n * rows * feats * hidden,
    )


def mlp_weights_kernel(plan_second, plan_out, *refs):
    a, b = len(plan_second), len(plan_out)
    second_refs, out_refs, refs = refs[:a], refs[a : a + b], refs[a + b :]
    active, back, g_up, g_down, s_up, s_down, held, sems = refs
    n, rows, feats = held.shape
    hidden = active.shape[2]
    load_chunks(plan_second, second_refs, held, sems)
    back_rows = back[...].reshape(n * rows, hidden)
    s_up[...] = jnp.sum(back_rows.astype(f32), axis=0, keepdims=True)
    g_up[...] = dot(held[...].reshape(n * rows, feats), back_rows, TN).astype(bf16)
    load_chunks(plan_out, out_refs, held, sems)
    out_rows = held[...].reshape(n * rows, feats)
    s_down[...] = jnp.sum(out_rows.astype(f32), axis=0, keepdims=True)
    g_down[...] = dot(active[...].reshape(n * rows, hidden), out_rows, TN).astype(bf16)


def mlp_weights(second_chunks, out_chunks, active, back):
    n, rows, hidden = active.shape
    feats = second_chunks[0][0].shape[1]
    outs = [
        sds((feats, hidden), bf16),
        sds((hidden, feats), bf16),
        sds((1, hidden), f32),
        sds((1, feats), f32),
    ]
    return call(
        functools.partial(mlp_weights_kernel, chunk_plan(second_chunks), chunk_plan(out_chunks)),
        "mlp_weights",
        second_chunks + out_chunks,
        [active, back],
        outs,
        [pltpu.VMEM((n, rows, feats), bf16)],
        4 * n * rows * feats * hidden,
    )


def normed(values):
    centered = values - jnp.mean(values, axis=-1, keepdims=True)
    inverse = lax.rsqrt(jnp.mean(centered * centered, axis=-1, keepdims=True) + epsilon)
    return centered * inverse, inverse


def norm_back(grad, scale, unit, inverse):
    g = grad * (1.0 + scale)
    mean_g = jnp.mean(g, axis=-1, keepdims=True)
    mean_gm = jnp.mean(g * unit, axis=-1, keepdims=True)
    return inverse * (g - mean_g - unit * mean_gm)


def exact(onehot, values):
    return jnp.dot(onehot.astype(f32), values, precision=highest)


def fetch_block(layer, params, place):
    _, _, qkv_weight, _, out_weight, _, up_weight, _, down_weight, _ = params
    n, nz, b, z, nh, hd = place
    mine = nh * hd
    shard, feats = out_weight.shape[1:]
    qkv = qkv_weight[layer].reshape(shard, 3, feats)
    qkv = lax.dynamic_slice_in_dim(qkv, b * mine, mine, 2).reshape(shard, 3 * mine)
    hidden = up_weight.shape[2] // (n * nz)
    up = up_weight[layer].reshape(shard, nz, n * hidden)
    up = lax.dynamic_slice_in_dim(up, b * hidden, hidden, 2).reshape(shard, nz * hidden)
    down = lax.dynamic_slice_in_dim(down_weight[layer], b * hidden, hidden, 0)
    start = b * mine
    out = lax.dynamic_slice_in_dim(out_weight[layer], start % shard, mine, 0)
    out = jnp.where(start // shard == z, out, jnp.zeros_like(out))
    return (
        lax.all_gather(qkv, "dp", axis=0, tiled=True),
        lax.psum(out, "dp"),
        lax.all_gather(up, "dp", axis=0, tiled=True),
        lax.all_gather(down, "dp", axis=0, tiled=True),
    )


def per_device(
    tokens,
    cond,
    segments,
    kept,
    cotangent,
    ada_weight,
    ada_bias,
    qkv_weight,
    qv_bias,
    out_weight,
    out_bias,
    up_weight,
    up_bias,
    down_weight,
    down_bias,
):
    params = (
        ada_weight,
        ada_bias,
        qkv_weight,
        qv_bias,
        out_weight,
        out_bias,
        up_weight,
        up_bias,
        down_weight,
        down_bias,
    )
    n, nz = lax.axis_size("blk"), lax.axis_size("dp")
    b, z = lax.axis_index("blk"), lax.axis_index("dp")
    rows, feats = tokens.shape
    keep = kept.shape[0]
    layers = ada_weight.shape[0]
    hd = feats // HEADS
    nh = HEADS // n
    mine = nh * hd
    scale = hd**-0.5
    images = cond.shape[0] // nz
    big = images // 5
    place = (n, nz, b, z, nh, hd)

    lengths = [BIG_LEN] * big + [SMALL_LEN] * (images - big)
    plan, off, base = [], 0, 0
    for length in lengths:
        plan.append((off, length // n, base))
        off += length // n
        base += length
    plan = tuple(plan)
    plan_kept = ((0, keep, 0),)

    silu_c = jax.nn.silu(cond.astype(f32)).astype(bf16)
    shard = ada_weight.shape[1]
    cond_rows = lax.dynamic_slice_in_dim(silu_c, z * shard, shard, 1)
    width = ada_weight.shape[2] // n
    ada_part = lax.dynamic_slice_in_dim(ada_weight, b * width, width, 2)
    partial = jnp.einsum("ik,lkc->lic", cond_rows, ada_part, preferred_element_type=f32)
    held = ada_bias.shape[1]
    bias_part = lax.dynamic_slice_in_dim(ada_bias, (b * width) % held, width, 1).astype(f32)
    partial = partial + jnp.where((b * width) // held == z, bias_part, 0.0)[:, None, :]
    partial = partial.reshape(layers, nz, images, width)
    mod = lax.dynamic_index_in_dim(partial, z, 1, keepdims=False)
    for s in range(1, nz):
        sent = lax.dynamic_index_in_dim(partial, (z + s) % nz, 1, keepdims=False)
        mod = mod + lax.ppermute(sent, "dp", [(i, (i + s) % nz) for i in range(nz)])
    mod = lax.all_gather(mod, "blk", axis=2, tiled=True)

    packed = jnp.concatenate([qv_bias, out_bias, up_bias, down_bias], axis=1)
    packed = lax.all_gather(packed, "dp", axis=0).astype(f32)
    sizes = [a.shape[1] for a in (qv_bias, out_bias, up_bias, down_bias)]
    cuts = [sum(sizes[:i]) for i in range(1, 4)]
    qv_all, out_all, up_all, down_all = jnp.split(packed, cuts, axis=2)
    qv_all = jnp.moveaxis(qv_all, 0, 1).reshape(layers, -1)
    out_all = jnp.moveaxis(out_all, 0, 1).reshape(layers, 1, -1)
    down_all = jnp.moveaxis(down_all, 0, 1).reshape(layers, 1, -1)
    hidden = up_bias.shape[1] // n
    up_mine = lax.dynamic_slice_in_dim(up_all, b * hidden, hidden, 2)
    up_mine = jnp.moveaxis(up_mine, 0, 1).reshape(layers, 1, -1)

    spread = jnp.arange(3 * mine, dtype=jnp.int32)
    spread = spread // hd * PAD + spread % hd
    spread = (spread[:, None] == jnp.arange(3 * nh * PAD, dtype=jnp.int32)[None, :]).astype(bf16)
    spread_out = spread[:mine, : nh * PAD]
    q_bias = lax.dynamic_slice_in_dim(qv_all, b * mine, mine, 1)
    v_bias = lax.dynamic_slice_in_dim(qv_all, feats + b * mine, mine, 1)
    ones = jnp.zeros((1, nh, PAD), f32).at[:, :, PAD_L : PAD_L + 2].set(1.0).reshape(1, nh * PAD)
    place_bias = lambda part: jnp.dot(part, spread_out.astype(f32), precision=highest)
    qkv_bias = jnp.concatenate(
        [
            place_bias(q_bias),
            jnp.zeros((layers, nh * PAD), f32),
            place_bias(v_bias) + ones,
        ],
        axis=1,
    ).reshape(layers, 1, -1)

    local = segments - z * images
    index = jnp.arange(rows, dtype=jnp.int32)
    before = (local[None, :] < local[:, None]) | (
        (local[None, :] == local[:, None]) & (index[None, :] < index[:, None])
    )
    rank = jnp.sum(before.astype(jnp.int32), axis=1)
    order = rank[None, :] == index[:, None]
    chosen = kept[:, None] == index[None, :]
    kept_rank = jnp.sum(jnp.where(chosen, rank[None, :], 0), axis=1)
    kept_local = jnp.sum(jnp.where(chosen, local[None, :], 0), axis=1)
    select = kept_rank[:, None] == index[None, :]
    is_kept = jnp.any(select, axis=0)[:, None]
    tok = jnp.dot(order.astype(bf16), tokens, preferred_element_type=f32)
    cot = jnp.dot(order.astype(bf16), cotangent, preferred_element_type=f32)
    cot_kept = jnp.dot(select.astype(bf16), cot.astype(bf16), preferred_element_type=f32)

    sorted_local = jnp.concatenate(
        [jnp.full((size,), i, jnp.int32) for i, (_, size, _) in enumerate(plan)]
    )
    image_ids = jnp.arange(images, dtype=jnp.int32)
    hot = (sorted_local[:, None] == image_ids[None, :]).astype(f32)
    hot_kept = (kept_local[:, None] == image_ids[None, :]).astype(f32)

    seg_chunks = gather_rows(kept_local, n)
    seg_pieces = {}
    for array, k, first in seg_chunks:
        seg_pieces.setdefault(k, []).append((first, array))
    seg_all = jnp.concatenate(
        [a for k in range(n) for _, a in sorted(seg_pieces[k], key=lambda item: item[0])]
    )
    segs = (seg_all[:, None], seg_all[None, :])

    fetched = [fetch_block(layer, params, place) for layer in range(layers)]

    def forward(layer, x, onehot, images_plan, seg_pair):
        wqkv, wout, wup, wdown = fetched[layer]
        wqkv = dot(wqkv, spread).astype(bf16)
        wout = dot(spread_out, wout, TN).astype(bf16)
        per_row = jnp.dot(onehot, mod[layer], precision=highest)
        shift1, scale1, gate1, shift2, scale2, gate2 = jnp.split(per_row, 6, axis=1)
        unit1, inv1 = normed(x)
        first = (unit1 * (1.0 + scale1) + shift1).astype(bf16)
        first_chunks = gather_rows(first, n)
        qkv, al, mixed, even, odd = attn_forward(
            first_chunks, wqkv, qkv_bias[layer], wout, seg_pair, n, images_plan, scale, nh
        )
        branch = reduce_rows(even, odd, n) + out_all[layer]
        middle = x + gate1 * branch
        unit2, inv2 = normed(middle)
        second = (unit2 * (1.0 + scale2) + shift2).astype(bf16)
        second_chunks = gather_rows(second, n)
        active, slope, even, odd = mlp_forward(second_chunks, wup, up_mine[layer], wdown, n)
        output = reduce_rows(even, odd, n) + down_all[layer]
        stored = (
            (wqkv, wout, wup, wdown),
            (scale1, gate1, scale2, gate2),
            (unit1, inv1, unit2, inv2),
            (first_chunks, second_chunks),
            (qkv, al, mixed, branch, active, slope, output),
        )
        return middle + gate2 * output, stored

    def backward(layer, stored, grad_out, onehot, images_plan, seg_pair):
        (
            (wqkv, wout, wup, wdown),
            (scale1, gate1, scale2, gate2),
            (unit1, inv1, unit2, inv2),
            (first_chunks, second_chunks),
            (qkv, al, mixed, branch, active, slope, output),
        ) = stored
        d_out = (gate2 * grad_out).astype(bf16)
        out_chunks = gather_rows(d_out, n)
        back, even, odd = mlp_backward(out_chunks, wup, wdown, slope)
        g_up, g_down, s_up, s_down = mlp_weights(second_chunks, out_chunks, active, back)
        d_second = reduce_rows(even, odd, n)
        d_middle = grad_out + norm_back(d_second, scale2, unit2, inv2)
        d_branch = (gate1 * d_middle).astype(bf16)
        back_chunks = gather_rows(d_branch, n)
        dqkv, s_qkv, even, odd = attn_backward(
            back_chunks, wqkv, wout, qkv, al, seg_pair, n, images_plan, scale, nh
        )
        g_qkv, g_out, s_out = attn_weights(
            first_chunks, back_chunks, dqkv, mixed, spread, nh, hd
        )
        d_first = reduce_rows(even, odd, n)
        grad_x = d_middle + norm_back(d_first, scale1, unit1, inv1)
        per_row = jnp.concatenate(
            [
                d_first,
                d_first * unit1,
                d_middle * branch,
                d_second,
                d_second * unit2,
                grad_out * output,
            ],
            axis=1,
        )
        grad_mod = jnp.einsum("ri,rm->im", onehot, per_row, precision=highest)
        s_qkv = s_qkv.reshape(3, nh, PAD)[:, :, :hd].reshape(3, mine)
        return grad_x, (g_qkv, g_out, g_up, g_down), (s_qkv, s_out, s_up, s_down, grad_mod)

    def finish(grads, sums):
        g_qkv, g_out, g_up, g_down = grads
        s_qkv, s_out, s_up, s_down, grad_mod = sums
        share = feats // nz
        g_qkv = lax.psum_scatter(g_qkv, "dp", scatter_dimension=0, tiled=True)
        g_up = lax.psum_scatter(g_up, "dp", scatter_dimension=0, tiled=True)
        g_down = lax.psum_scatter(g_down, "dp", scatter_dimension=0, tiled=True)
        g_out = lax.psum(g_out, "dp")
        g_qkv = lax.all_gather(g_qkv, "blk", axis=0).reshape(n, share, 3, mine)
        g_qkv = jnp.transpose(g_qkv, (1, 2, 0, 3)).reshape(share, 3 * feats).astype(f32)
        g_up = lax.all_gather(g_up, "blk", axis=0).reshape(n, share, nz, hidden)
        g_up = jnp.transpose(g_up, (1, 2, 0, 3)).reshape(share, -1).astype(f32)
        g_down = lax.all_gather(g_down, "blk", axis=0, tiled=True).astype(f32)
        g_out = lax.all_gather(g_out, "blk", axis=0, tiled=True)
        g_out = lax.dynamic_slice_in_dim(g_out, z * share, share, 0).astype(f32)
        grad_mod = lax.psum(grad_mod, "blk")
        grad_mod = lax.all_gather(grad_mod, "dp", axis=0, tiled=True)
        g_ada = jnp.dot(cond_rows.astype(f32).T, grad_mod, precision=highest)
        ada_share = ada_bias.shape[1]
        sum_ada = lax.dynamic_slice_in_dim(jnp.sum(grad_mod, axis=0), z * ada_share, ada_share, 0)
        parts = jnp.concatenate([s_up.reshape(-1), s_qkv[0], s_qkv[2]])
        parts = lax.all_gather(parts, "blk", axis=0)
        up_sum = parts[:, : nz * hidden].reshape(n, nz, hidden)
        up_sum = jnp.transpose(up_sum, (1, 0, 2)).reshape(nz, -1)
        q_sum = parts[:, nz * hidden : nz * hidden + mine].reshape(-1)
        v_sum = parts[:, nz * hidden + mine :].reshape(-1)
        qv_sum = jnp.concatenate([q_sum, v_sum]).reshape(nz, -1)
        line = jnp.concatenate(
            [up_sum, qv_sum, s_out.reshape(nz, -1), s_down.reshape(nz, -1)], axis=1
        )
        line = lax.psum(line, "dp")
        line = lax.dynamic_index_in_dim(line, z, 0, keepdims=False)
        widths = [up_sum.shape[1], qv_sum.shape[1], share]
        at = [sum(widths[: i + 1]) for i in range(3)]
        up_line, qv_line, out_line, down_line = jnp.split(line, at)
        return (
            g_ada,
            sum_ada,
            g_qkv,
            qv_line,
            g_out,
            out_line,
            g_up,
            up_line,
            g_down,
            down_line,
        )

    mid, stored0 = forward(0, tok, hot, plan, None)
    mid_kept = exact(select, mid)
    routed, stored1 = forward(1, mid_kept, hot_kept, plan_kept, segs)
    grad_kept, grads1, sums1 = backward(1, stored1, cot_kept, hot_kept, plan_kept, segs)
    out1 = finish(grads1, sums1)
    spread_back = exact(select.T, grad_kept)
    grad_mid = jnp.where(is_kept, spread_back, cot)
    grad_tok, grads0, sums0 = backward(0, stored0, grad_mid, hot, plan, None)
    out0 = finish(grads0, sums0)
    back_order = order.T
    mid_out = exact(back_order, mid)
    final = exact(chosen.T, routed)
    final = jnp.where(jnp.any(chosen, axis=0)[:, None], final, mid_out)
    grad_tokens = exact(back_order, grad_tok)
    stacked = tuple(jnp.stack([a0, a1]) for a0, a1 in zip(out0, out1))
    return (mid_out, final, grad_tokens) + stacked


def solution(mesh):
    return jax.shard_map(
        per_device,
        mesh=mesh,
        in_specs=(
            P(("dp", "blk"), None),
            P(),
            P(("dp", "blk")),
            P(("dp", "blk")),
            P(("dp", "blk"), None),
            P(None, "dp", None),
            P(None, "dp"),
            P(None, "dp", None),
            P(None, "dp"),
            P(None, "dp", None),
            P(None, "dp"),
            P(None, "dp", None),
            P(None, "dp"),
            P(None, "dp", None),
            P(None, "dp"),
        ),
        out_specs=(
            P(("dp", "blk"), None),
            P(("dp", "blk"), None),
            P(("dp", "blk"), None),
            P(None, "dp", None),
            P(None, "dp"),
            P(None, "dp", None),
            P(None, "dp"),
            P(None, "dp", None),
            P(None, "dp"),
            P(None, "dp", None),
            P(None, "dp"),
            P(None, "dp", None),
            P(None, "dp"),
        ),
        check_vma=False,
    )
```

time: 4090 us -> 1220 us (0.30)
  waiting for transfers between devices: 3100 us -> 338 us
  matrix products: 568 us -> 51.6 us
  Pallas kernels: 0 us -> 195 us
  starting transfers between devices: 1.4 us -> 99 us
  local copies, waits for them, and re-layouts: 137 us -> 215 us
    all_gather x18 -> x12, waiting for transfers between devices: 1480 us -> 111 us  [the longest x2 56 us: finish(): g_out = lax.all_gather(g_out, 'blk', axis=0, tiled=True)]
    reduce_scatter x10 -> x6, waiting for transfers between devices: 1360 us -> 0.06 us  [the longest x2 0.03 us: finish(): g_down = lax.psum_scatter(g_down, 'dp', scatter_dimension=0, tiled=True)]
    dot_general x144 -> x21, matrix products: 568 us -> 51.6 us  [the longest x5 12.5 us: exact(): return jnp.dot(onehot.astype(f32), values, precision=highest)]
    psum x1 -> x4, waiting for transfers between devices: 254 us -> 49 us  [the longest x1 48.9 us: finish(): grad_mod = lax.psum(grad_mod, 'blk')]
    pallas_call x0 -> x12, Pallas kernels: none -> 195 us  [call(): pl.pallas_call(kernel, name=name, out_shape=outs, in_specs=[pl.BlockSpec(...]
    ppermute x0 -> x140, waiting for transfers between devices: none -> 174 us  [the longest x137 174 us: swap(): return lax.ppermute(x, 'blk', [(i, i ^ bit) for i in range(n)])]
    ppermute x0 -> x140, starting transfers between devices: none -> 96.8 us  [the longest x137 90.7 us: swap(): return lax.ppermute(x, 'blk', [(i, i ^ bit) for i in range(n)])]
    all_gather x6, blocking collectives: 72.8 us -> 145 us  [the longest x2 56 us: fetch_block(): lax.all_gather(qkv, 'dp', axis=0, tiled=True)]
  transfers between devices with their start and end apart: 29 -> 162, of which waited for: 20 -> 71; matrix products, arithmetic and copies ran while one was open for 18% -> 28% of each run, Pallas kernels for 0% -> 9%
where the time goes in v1:
time: 1220 us; the launch traced here: 1210 us
  waiting for transfers between devices  338 us (28%)
  local copies, waits for them, and re-layouts  215 us (18%)
  Pallas kernels  195 us (16%)
  blocking collectives  170 us (14%)
  other arithmetic  127 us (10%)
  starting transfers between devices  99 us (8%)
  matrix products  51.6 us (4%)
  between operations  17.9 us (1%)
    pallas_call x12, Pallas kernels, call(): pl.pallas_call(kernel, name=name, out_shape=outs, in_specs=[pl.BlockSpec(...  195 us
    ppermute x137, waiting for transfers between devices, swap(): return lax.ppermute(x, 'blk', [(i, i ^ bit) for i in range(n)])  174 us
    ppermute x137, starting transfers between devices, swap(): return lax.ppermute(x, 'blk', [(i, i ^ bit) for i in range(n)])  90.7 us
    all_gather x2, blocking collectives, fetch_block(): lax.all_gather(qkv, 'dp', axis=0, tiled=True)  56 us
    all_gather x2, waiting for transfers between devices, finish(): g_out = lax.all_gather(g_out, 'blk', axis=0, tiled=True)  56 us
    psum x1, waiting for transfers between devices, finish(): grad_mod = lax.psum(grad_mod, 'blk')  48.9 us
    all_gather x2, blocking collectives, finish(): grad_mod = lax.all_gather(grad_mod, 'dp', axis=0, tiled=True)  39.3 us
    unnamed x303, local copies, waits for them, and re-layouts  38.4 us
  transfers between devices with their start and end apart: 162, of which 71 were waited for; matrix products, arithmetic and copies ran while one was open for 28% of the time, Pallas kernels for 9%

profile of v1, /device:TPU:0, one launch (start us, length us, event | category | flops | bytes accessed | tf_op | source)
XLA Modules:
  0.0 1212.6 jit_solution(14054975429457495146)
XLA Ops:
  26.0 5.0 reshape_squeeze.14
  30.9 5.0 reshape_squeeze.12
  39.0 33.7 %all_gather.82 = bf16[1152,432]{1,0:T(8,128)(2,1)} all-gather(bf16[288,432]{1,0:T(8,128)(2,1)S(1)} %copy.108), channel_id=1, replica_groups=mesh['dp'=4,'blk'=8] {'dp'}, dimensions={0}, use_global_device_ids=true | all-gather | bytes 1244160 | tf_op jit(solution)/shard_map/all_gather | solution.py:510
  73.1 13.8 %all-gather.9 = bf16[4,2,2304]{2,1,0:T(2,128)(2,1)} all-gather(bf16[1,2,2304]{2,1,0:T(2,128)(2,1)S(1)} %bitcast.379), channel_id=2, replica_groups=mesh['dp'=4,'blk'=8] {'dp'}, dimensions={0}, use_global_device_ids=true | all-gather | bytes 46080 | tf_op jit(solution)/shard_map/all_gather | solution.py:585
  88.1 35.8 %all_gather.81 = f32[2,5,6912]{1,0,2:T(2,128)S(1)} all-gather(f32[2,5,864]{1,0,2:T(2,128)S(1)} %copy.106), channel_id=1, replica_groups=mesh['dp'=4,'blk'=8] {'blk'}, dimensions={2}, use_global_device_ids=true | all-gather | bytes 311040 | tf_op jit(solution)/shard_map/all_gather | solution.py:582
  123.9 6.4 fusion.165
  145.1 7.5 collective-permute-done.6.refs_4_
  167.2 23.5 %attn_forward.2 = (bf16[6,2048,128]{2,1,0:T(8,128)(2,1)}, f32[2,2048,128]{2,1,0:T(8,128)}, bf16[8,256,256]{2,1,0:T(8,128)(2,1)}, bf16[4,256,1152]{2,1,0:T(8,128)(2,1)}, bf16[4,256,1152]{2,1,0:T(8,128)(2,1)}) custom-call(bf16[256,1152]{1,0:T(8,128)(2,1)} %copy-done.46, bf16[256,1152]{1,0:T(8,128)(2,1)} %copy-done.113, ...), custom_call_target="tpu_custom_call" | custom-call | flops 9126805504 | bytes 18091008 | tf_op jit(solution)/shard_map/attn_forward/pallas_call | solution.py:113
  206.5 5.3 fusion.153
  243.9 11.8 collective-permute-done.22.refs_4_
  269.5 5.3 all-gather.37.cloned.1.call-done
  274.8 18.2 %mlp_forward.2 = (bf16[8,256,576]{2,1,0:T(8,128)(2,1)}, bf16[8,256,576]{2,1,0:T(8,128)(2,1)}, bf16[4,256,1152]{2,1,0:T(8,128)(2,1)}, bf16[4,256,1152]{2,1,0:T(8,128)(2,1)}) custom-call(bf16[256,1152]{1,0:T(8,128)(2,1)} %copy-done.47, bf16[256,1152]{1,0:T(8,128)(2,1)} %collective-permute-done.19.refs_1_, bf16[256,1152]{1,0:T(8,128)(2,1)} %collective-permute-done.20.refs_2_, ...), custom_call_target="tpu_custom_call" | custom-call | flops 5435817984 | bytes 16812288 | tf_op jit(solution)/shard_map/mlp_forward/pallas_call | solution.py:113
  293.2 4.7 collective-permute-done.28
  333.9 22.3 %all_gather.87 = bf16[1152,432]{1,0:T(8,128)(2,1)S(1)} all-gather(bf16[288,432]{1,0:T(8,128)(2,1)S(1)} %copy-done.45), channel_id=1, replica_groups=mesh['dp'=4,'blk'=8] {'dp'}, dimensions={0}, use_global_device_ids=true | all-gather | bytes 1244160 | tf_op jit(solution)/shard_map/all_gather | solution.py:510
  373.4 14.8 %attn_forward.3 = (bf16[6,1024,128]{2,1,0:T(8,128)(2,1)}, f32[2,1024,128]{2,1,0:T(8,128)}, bf16[8,128,256]{2,1,0:T(8,128)(2,1)}, bf16[4,128,1152]{2,1,0:T(8,128)(2,1)}, bf16[4,128,1152]{2,1,0:T(8,128)(2,1)}) custom-call(bf16[128,1152]{1,0:T(8,128)(2,1)} %fusion.34.refs_0_, bf16[128,1152]{1,0:T(8,128)(2,1)} %collective-permute-done.35.refs_1_, ...), custom_call_target="tpu_custom_call" | custom-call | flops 3489660928 | bytes 10234880 | tf_op jit(solution)/shard_map/attn_forward/pallas_call | solution.py:113
  420.0 6.2 collective-permute-done.79.refs_4_.refs_14_
  445.4 12.2 %all-gather.39.cloned.1.call-done = bf16[1,576,1152]{2,1,0:T(8,128)(2,1)} async-done(((bf16[1,144,1152]{2,1,0:T(8,128)(2,1)}), bf16[1,576,1152]{2,1,0:T(8,128)(2,1)}) %all-gather.39.cloned.1.call-update) | async-done | bytes 1327120 | tf_op jit(solution)/shard_map/all_gather | solution.py:513
  457.6 12.0 mlp_forward.3
  469.8 12.4 %mlp_backward.2 = (bf16[8,128,576]{2,1,0:T(8,128)(2,1)}, bf16[4,128,1152]{2,1,0:T(8,128)(2,1)}, bf16[4,128,1152]{2,1,0:T(8,128)(2,1)}) custom-call(bf16[128,1152]{1,0:T(8,128)(2,1)} %get-tuple-element.235.refs_0_.refs_10_, bf16[128,1152]{1,0:T(8,128)(2,1)} %collective-permute-done.76.refs_1_.refs_11_, ...), custom_call_target="tpu_custom_call" | custom-call | flops 2717908992 | bytes 9732096 | tf_op jit(solution)/shard_map/mlp_backward/pallas_call | solution.py:113
  519.8 21.9 %attn_backward.2 = (bf16[8,128,768]{2,1,0:T(8,128)(2,1)}, f32[1,768]{1,0:T(1,128)}, bf16[4,128,1152]{2,1,0:T(8,128)(2,1)}, bf16[4,128,1152]{2,1,0:T(8,128)(2,1)}) custom-call(bf16[128,1152]{1,0:T(8,128)(2,1)} %copy-done.55, bf16[128,1152]{1,0:T(8,128)(2,1)} %copy-done.123, bf16[128,1152]{1,0:T(8,128)(2,1)} %copy-done.65, bf16[128,1152]{1,0:T(8,128)(2,1)} %copy-done.125, ...), custom_call_target="tpu_custom_call" | custom-call | flops 5100273664 | bytes 11283456 | tf_op jit(solution)/shard_map/attn_backward/pallas_call | solution.py:113
  558.4 9.1 mlp_weights.3
  576.6 11.8 collective-permute-done.111.refs_4_.refs_14_
  598.9 16.3 %mlp_backward.3 = (bf16[8,256,576]{2,1,0:T(8,128)(2,1)}, bf16[4,256,1152]{2,1,0:T(8,128)(2,1)}, bf16[4,256,1152]{2,1,0:T(8,128)(2,1)}) custom-call(bf16[256,1152]{1,0:T(8,128)(2,1)} %copy-done.48, bf16[256,1152]{1,0:T(8,128)(2,1)} %copy-done.114, bf16[256,1152]{1,0:T(8,128)(2,1)} %copy-done.62, bf16[256,1152]{1,0:T(8,128)(2,1)} %copy-done.116, ...), custom_call_target="tpu_custom_call" | custom-call | flops 5435817984 | bytes 16809984 | tf_op jit(solution)/shard_map/mlp_backward/pallas_call | solution.py:113
  615.4 9.3 attn_weights.3
  625.0 14.6 %mlp_weights.2 = (bf16[1152,576]{1,0:T(8,128)(2,1)}, bf16[576,1152]{1,0:T(8,128)(2,1)}, f32[1,576]{1,0:T(1,128)}, f32[1,1152]{1,0:T(1,128)}) custom-call(bf16[256,1152]{1,0:T(8,128)(2,1)} %copy-done.47, bf16[256,1152]{1,0:T(8,128)(2,1)} %collective-permute-done.19.refs_1_, bf16[256,1152]{1,0:T(8,128)(2,1)} %collective-permute-done.20.refs_2_, ...), custom_call_target="tpu_custom_call" | custom-call | flops 5435817984 | bytes 16816896 | tf_op jit(solution)/shard_map/mlp_weights/pallas_call | solution.py:113
  647.8 5.8 collective-permute-done.121
  675.9 13.5 %collective-permute-done.127.refs_4_.refs_14_ = bf16[256,1152]{1,0:T(8,128)(2,1)} collective-permute-done((bf16[256,1152]{1,0:T(8,128)(2,1)}, bf16[256,1152]{1,0:T(8,128)(2,1)}, u32[]{:S(2)}, u32[]{:S(2)}) %collective-permute-start.127) | collective-permute-done | bytes 589856 | tf_op jit(solution)/shard_map/ppermute | solution.py:31
  701.4 28.9 %attn_backward.3 = (bf16[8,256,768]{2,1,0:T(8,128)(2,1)}, f32[1,768]{1,0:T(1,128)}, bf16[4,256,1152]{2,1,0:T(8,128)(2,1)}, bf16[4,256,1152]{2,1,0:T(8,128)(2,1)}) custom-call(bf16[256,1152]{1,0:T(8,128)(2,1)} %get-tuple-element.195.refs_0_.refs_10_, bf16[256,1152]{1,0:T(8,128)(2,1)} %copy-done.117, ...), custom_call_target="tpu_custom_call" | custom-call | flops 15569256448 | bytes 20188160 | tf_op jit(solution)/shard_map/attn_backward/pallas_call | solution.py:113
  730.3 13.8 %attn_weights.2 = (bf16[1152,432]{1,0:T(8,128)(2,1)}, bf16[144,1152]{1,0:T(8,128)(2,1)}, f32[1,1152]{1,0:T(1,128)}) custom-call(bf16[256,1152]{1,0:T(8,128)(2,1)} %copy-done.46, bf16[256,1152]{1,0:T(8,128)(2,1)} %copy-done.113, bf16[256,1152]{1,0:T(8,128)(2,1)} %collective-permute-done.4.refs_2_, bf16[256,1152]{1,0:T(8,128)(2,1)} %collective-permute-done.5.refs_3_, ...), custom_call_target="tpu_custom_call" | custom-call | flops 4831838208 | bytes 15626752 | tf_op jit(solution)/shard_map/attn_weights/pallas_call | solution.py:113
  797.2 24.9 %all-reduce.2 = (f32[6912]{0:T(1024)}, f32[6912]{0:T(1024)}) all-reduce(f32[6912]{0:T(1024)} %maximum_dynamic-update-slice_fusion.1, f32[6912]{0:T(1024)} %maximum_dynamic-update-slice_fusion), channel_id=8, replica_groups=mesh['dp'=4,'blk'=8] {'blk'}, use_global_device_ids=true, to_apply=%add.1 | all-reduce | flops 13824 | bytes 110592
  826.4 5.2 fusion.156
  898.2 7.9 convert_element_type.589
  914.5 6.3 convert_element_type.583
  935.9 48.9 %all-reduce.12.cloned.1.call-done = (f32[5,6912]{1,0:T(8,128)}, f32[5,6912]{1,0:T(8,128)}) async-done(((f32[5,6912]{1,0:T(8,128)}, f32[5,6912]{1,0:T(8,128)}), (f32[5,6912]{1,0:T(8,128)}, f32[5,6912]{1,0:T(8,128)})) %all-reduce.12.cloned.1.call-update) | async-done | bytes 276496 | tf_op jit(solution)/shard_map/psum | solution.py:729
  984.9 21.1 %all-gather.10 = f32[4,5,6912]{2,1,0:T(8,128)S(1)} all-gather(f32[1,5,6912]{2,1,0:T(8,128)} %bitcast.376), channel_id=1, replica_groups=mesh['dp'=4,'blk'=8] {'dp'}, dimensions={0}, use_global_device_ids=true | all-gather | bytes 691200 | tf_op jit(solution)/shard_map/all_gather | solution.py:730
  1006.1 18.2 %all-gather.11 = f32[4,5,6912]{2,1,0:T(8,128)S(1)} all-gather(f32[1,5,6912]{2,1,0:T(8,128)S(1)} %bitcast.375), channel_id=1, replica_groups=mesh['dp'=4,'blk'=8] {'dp'}, dimensions={0}, use_global_device_ids=true | all-gather | bytes 691200 | tf_op jit(solution)/shard_map/all_gather | solution.py:730
  1031.2 6.3 pad_maximum_fusion
  1043.1 7.9 convert_element_type.586
  1054.1 6.5 maximum_convert_fusion
  1060.6 12.5 %copy.129 = f32[2,288,4608]{2,1,0:T(8,128)} copy(f32[2,288,4608]{1,2,0:T(8,128)} %maximum_convert_fusion) | data formatting | bytes 21233664
  1073.0 9.1 all-gather.33.cloned.1.call-done
  1082.1 7.4 maximum_convert_fusion.2
  1089.5 24.8 %all-gather.31.cloned.1.call-done = bf16[1152,1152]{1,0:T(8,128)(2,1)} async-done(((bf16[144,1152]{1,0:T(8,128)(2,1)}), bf16[1152,1152]{1,0:T(8,128)(2,1)}) %all-gather.31.cloned.1.call-update) | async-done | bytes 2654224 | tf_op jit(solution)/shard_map/all_gather | solution.py:727
  1115.4 31.2 %all-gather.29.cloned.1.call-done = bf16[1152,1152]{1,0:T(8,128)(2,1)} async-done(((bf16[144,1152]{1,0:T(8,128)(2,1)}), bf16[1152,1152]{1,0:T(8,128)(2,1)}) %all-gather.29.cloned.1.call-update) | async-done | bytes 2654224 | tf_op jit(solution)/shard_map/all_gather | solution.py:727
  1149.4 28.3 %all-gather.41.cloned.1.call-done = bf16[2304,432]{1,0:T(8,128)(2,1)} async-done(((bf16[288,432]{1,0:T(8,128)(2,1)}), bf16[2304,432]{1,0:T(8,128)(2,1)}) %all-gather.41.cloned.1.call-update) | async-done | bytes 1990672 | tf_op jit(solution)/shard_map/all_gather | solution.py:722
  1181.8 6.3 convert_element_type.580
  1190.6 5.0 maximum_convert_fusion.1
  1195.7 9.6 copy.128
  (863 shorter events, 506.3 us)
Async XLA Ops:
  7.2 156.9 %all-reduce.18.cloned.1.call-start = ((), (), s32[]{:S(2)}) async-start(), calls=%async_computation.27 | async-start | bytes 1327104 | tf_op jit(solution)/shard_map/psum | solution.py:511
  11.0 76.0 %collective-permute-start = (f32[2,5,864]{2,0,1:T(2,128)S(1)}, f32[2,5,864]{2,0,1:T(2,128)S(1)}, u32[]{:S(2)}, u32[]{:S(2)}) collective-permute-start(f32[2,5,864]{2,0,1:T(2,128)S(1)} %get-tuple-element.297), channel_id=1, source_target_pairs={{0,8},{8,16},{16,24},{24,0},{1,9},{9,17},{17,25},{25,1},{2,10},{10... | collective-permute-start | bytes 103688 | tf_op jit(solution)/shard_map/ppermute | solution.py:581
  14.0 72.9 %collective-permute-start.2 = (f32[2,5,864]{2,0,1:T(2,128)S(1)}, f32[2,5,864]{2,0,1:T(2,128)S(1)}, u32[]{:S(2)}, u32[]{:S(2)}) collective-permute-start(f32[2,5,864]{2,0,1:T(2,128)S(1)} %get-tuple-element.298), channel_id=1, source_target_pairs={{0,24},{8,0},{16,8},{24,16},{1,25},{9,1},{17,9},{25,17},{2,26},{10... | collective-permute-start | bytes 103688 | tf_op jit(solution)/shard_map/ppermute | solution.py:581
  16.1 70.8 %collective-permute-start.1 = (f32[2,5,864]{2,0,1:T(2,128)S(1)}, f32[2,5,864]{2,0,1:T(2,128)S(1)}, u32[]{:S(2)}, u32[]{:S(2)}) collective-permute-start(f32[2,5,864]{2,0,1:T(2,128)S(1)} %get-tuple-element.299), channel_id=1, source_target_pairs={{0,16},{8,24},{16,0},{24,8},{1,17},{9,25},{17,1},{25,9},{2,18},{10... | collective-permute-start | bytes 103688 | tf_op jit(solution)/shard_map/ppermute | solution.py:581
  19.6 249.9 %all-gather.25.cloned.1.call-start = ((), (), s32[]{:S(2)}) async-start(), calls=%async_computation.6 | async-start | bytes 1843200 | tf_op jit(solution)/shard_map/all_gather | solution.py:512
  137.1 16.9 %collective-permute-start.4 = (bf16[256,1152]{1,0:T(8,128)(2,1)S(1)}, bf16[256,1152]{1,0:T(8,128)(2,1)}, u32[]{:S(2)}, u32[]{:S(2)}) collective-permute-start(bf16[256,1152]{1,0:T(8,128)(2,1)S(1)} %fusion.1.refs_0_), channel_id=1, source_target_pairs={{0,2},{1,3},{2,0},{3,1},{4,6},{5,7},{6,4},{7,5},{8,10},{9,11},{10,... | collective-permute-start | bytes 1769480 | tf_op jit(solution)/shard_map/ppermute | solution.py:31
  206.3 68.5 %all-gather.37.cloned.1.call-start = ((), (), s32[]{:S(2)}) async-start(), calls=%async_computation.18 | async-start | bytes 1658880 | tf_op jit(solution)/shard_map/all_gather | solution.py:513
  217.5 227.9 %all-gather.27.cloned.1.call-start = ((), (), s32[]{:S(2)}) async-start(), calls=%async_computation.7 | async-start | bytes 1843200 | tf_op jit(solution)/shard_map/all_gather | solution.py:512
  243.9 30.9 %collective-permute-start.19 = (bf16[256,1152]{1,0:T(8,128)(2,1)S(1)}, bf16[256,1152]{1,0:T(8,128)(2,1)}, u32[]{:S(2)}, u32[]{:S(2)}) collective-permute-start(bf16[256,1152]{1,0:T(8,128)(2,1)S(1)} %fusion.refs_0_), channel_id=1, source_target_pairs={{0,1},{1,0},{2,3},{3,2},{4,5},{5,4},{6,7},{7,6},{8,9},{9,8},{10,11... | collective-permute-start | bytes 1769480 | tf_op jit(solution)/shard_map/ppermute | solution.py:31
  257.3 17.5 %collective-permute-start.23 = (bf16[256,1152]{1,0:T(8,128)(2,1)}, bf16[256,1152]{1,0:T(8,128)(2,1)}, u32[]{:S(2)}, u32[]{:S(2)}) collective-permute-start(bf16[256,1152]{1,0:T(8,128)(2,1)} %collective-permute-done.22.refs_4_), channel_id=1, source_target_pairs={{0,1},{1,0},{2,3},{3,2},{4,5},{5,4},{6,7},{7,6},{8,9},{9,8},{10,11... | collective-permute-start | bytes 1769480 | tf_op jit(solution)/shard_map/ppermute | solution.py:31
  258.3 16.5 %collective-permute-start.21 = (bf16[256,1152]{1,0:T(8,128)(2,1)}, bf16[256,1152]{1,0:T(8,128)(2,1)}, u32[]{:S(2)}, u32[]{:S(2)}) collective-permute-start(bf16[256,1152]{1,0:T(8,128)(2,1)} %collective-permute-done.20.refs_2_), channel_id=1, source_target_pairs={{0,1},{1,0},{2,3},{3,2},{4,5},{5,4},{6,7},{7,6},{8,9},{9,8},{10,11... | collective-permute-start | bytes 1769480 | tf_op jit(solution)/shard_map/ppermute | solution.py:31
  307.2 49.0 %collective-permute-start.47 = (s32[128]{0:T(128)}, s32[128]{0:T(128)S(1)}, u32[]{:S(2)}, u32[]{:S(2)}) collective-permute-start(s32[128]{0:T(128)} %get-tuple-element.183), channel_id=1, source_target_pairs={{0,4},{1,5},{2,6},{3,7},{4,0},{5,1},{6,2},{7,3},{8,12},{9,13},{10,... | collective-permute-start | bytes 1544 | tf_op jit(solution)/shard_map/ppermute | solution.py:31
  323.0 33.7 %collective-permute-start.45 = (s32[128]{0:T(128)}, s32[128]{0:T(128)S(1)}, u32[]{:S(2)}, u32[]{:S(2)}) collective-permute-start(s32[128]{0:T(128)} %get-tuple-element.183), channel_id=1, source_target_pairs={{0,2},{1,3},{2,0},{3,1},{4,6},{5,7},{6,4},{7,5},{8,10},{9,11},{10,... | collective-permute-start | bytes 1544 | tf_op jit(solution)/shard_map/ppermute | solution.py:31
  323.6 38.8 %collective-permute-start.44 = (s32[128]{0:T(128)}, s32[128]{0:T(128)S(1)}, u32[]{:S(2)}, u32[]{:S(2)}) collective-permute-start(s32[128]{0:T(128)} %get-tuple-element.183), channel_id=1, source_target_pairs={{0,1},{1,0},{2,3},{3,2},{4,5},{5,4},{6,7},{7,6},{8,9},{9,8},{10,11... | collective-permute-start | bytes 1544 | tf_op jit(solution)/shard_map/ppermute | solution.py:31
  331.8 26.3 %collective-permute-start.38 = (bf16[128,1152]{1,0:T(8,128)(2,1)}, bf16[128,1152]{1,0:T(8,128)(2,1)}, u32[]{:S(2)}, u32[]{:S(2)}) collective-permute-start(bf16[128,1152]{1,0:T(8,128)(2,1)} %fusion.34.refs_0_), channel_id=1, source_target_pairs={{0,4},{1,5},{2,6},{3,7},{4,0},{5,1},{6,2},{7,3},{8,12},{9,13},{10,... | collective-permute-start | bytes 884744 | tf_op jit(solution)/shard_map/ppermute | solution.py:31
  332.4 27.9 %collective-permute-start.36 = (bf16[128,1152]{1,0:T(8,128)(2,1)}, bf16[128,1152]{1,0:T(8,128)(2,1)}, u32[]{:S(2)}, u32[]{:S(2)}) collective-permute-start(bf16[128,1152]{1,0:T(8,128)(2,1)} %fusion.34.refs_0_), channel_id=1, source_target_pairs={{0,2},{1,3},{2,0},{3,1},{4,6},{5,7},{6,4},{7,5},{8,10},{9,11},{10,... | collective-permute-start | bytes 884744 | tf_op jit(solution)/shard_map/ppermute | solution.py:31
  389.4 68.3 %all-gather.39.cloned.1.call-start = ((), (), s32[]{:S(2)}) async-start(), calls=%async_computation.19 | async-start | bytes 1658880 | tf_op jit(solution)/shard_map/all_gather | solution.py:513
  399.1 345.2 %reduce-scatter.13.cloned.1.call-start = ((), (), s32[]{:S(2)}) async-start(), calls=%async_computation.13 | async-start | bytes 1843200 | tf_op jit(solution)/shard_map/reduce_scatter | solution.py:719
  443.0 26.7 %collective-permute-start.76 = (bf16[128,1152]{1,0:T(8,128)(2,1)}, bf16[128,1152]{1,0:T(8,128)(2,1)}, u32[]{:S(2)}, u32[]{:S(2)}) collective-permute-start(bf16[128,1152]{1,0:T(8,128)(2,1)} %get-tuple-element.235.refs_0_.refs_10_), channel_id=1, source_target_pairs={{0,1},{1,0},{2,3},{3,2},{4,5},{5,4},{6,7},{7,6},{8,9},{9,8},{10,11... | collective-permute-start | bytes 884744 | tf_op jit(solution)/shard_map/ppermute | solution.py:31
  443.0 26.7 %collective-permute-start.80 = (bf16[128,1152]{1,0:T(8,128)(2,1)}, bf16[128,1152]{1,0:T(8,128)(2,1)}, u32[]{:S(2)}, u32[]{:S(2)}) collective-permute-start(bf16[128,1152]{1,0:T(8,128)(2,1)} %collective-permute-done.79.refs_4_.refs_14_), channel_id=1, source_target_pairs={{0,1},{1,0},{2,3},{3,2},{4,5},{5,4},{6,7},{7,6},{8,9},{9,8},{10,11... | collective-permute-start | bytes 884744 | tf_op jit(solution)/shard_map/ppermute | solution.py:31
  443.5 26.3 %collective-permute-start.78 = (bf16[128,1152]{1,0:T(8,128)(2,1)}, bf16[128,1152]{1,0:T(8,128)(2,1)}, u32[]{:S(2)}, u32[]{:S(2)}) collective-permute-start(bf16[128,1152]{1,0:T(8,128)(2,1)} %collective-permute-done.77.refs_2_.refs_12_), channel_id=1, source_target_pairs={{0,1},{1,0},{2,3},{3,2},{4,5},{5,4},{6,7},{7,6},{8,9},{9,8},{10,11... | collective-permute-start | bytes 884744 | tf_op jit(solution)/shard_map/ppermute | solution.py:31
  444.9 24.8 %collective-permute-start.83 = (bf16[64,1152]{1,0:T(8,128)(2,1)}, bf16[64,1152]{1,0:T(8,128)(2,1)}, u32[]{:S(2)}, u32[]{:S(2)}) collective-permute-start(bf16[64,1152]{1,0:T(8,128)(2,1)} %copy-done.136), channel_id=1, source_target_pairs={{0,1},{1,0},{2,3},{3,2},{4,5},{5,4},{6,7},{7,6},{8,9},{9,8},{10,11... | collective-permute-start | bytes 442376 | tf_op jit(solution)/shard_map/ppermute | solution.py:31
  445.0 24.8 %collective-permute-start.84 = (bf16[64,1152]{1,0:T(8,128)(2,1)}, bf16[64,1152]{1,0:T(8,128)(2,1)}, u32[]{:S(2)}, u32[]{:S(2)}) collective-permute-start(bf16[64,1152]{1,0:T(8,128)(2,1)} %copy-done.138), channel_id=1, source_target_pairs={{0,1},{1,0},{2,3},{3,2},{4,5},{5,4},{6,7},{7,6},{8,9},{9,8},{10,11... | collective-permute-start | bytes 442376 | tf_op jit(solution)/shard_map/ppermute | solution.py:31
  550.0 17.7 %collective-permute-start.102 = (bf16[64,1152]{1,0:T(8,128)(2,1)}, bf16[64,1152]{1,0:T(8,128)(2,1)}, u32[]{:S(2)}, u32[]{:S(2)}) collective-permute-start(bf16[64,1152]{1,0:T(8,128)(2,1)} %get-tuple-element.281), channel_id=1, source_target_pairs={{0,2},{1,3},{2,0},{3,1},{4,6},{5,7},{6,4},{7,5},{8,10},{9,11},{10,... | collective-permute-start | bytes 442376 | tf_op jit(solution)/shard_map/ppermute | solution.py:31
  550.5 17.1 %collective-permute-start.107 = (bf16[64,1152]{1,0:T(8,128)(2,1)}, bf16[64,1152]{1,0:T(8,128)(2,1)}, u32[]{:S(2)}, u32[]{:S(2)}) collective-permute-start(bf16[64,1152]{1,0:T(8,128)(2,1)} %get-tuple-element.282), channel_id=1, source_target_pairs={{0,4},{1,5},{2,6},{3,7},{4,0},{5,1},{6,2},{7,3},{8,12},{9,13},{10,... | collective-permute-start | bytes 442376 | tf_op jit(solution)/shard_map/ppermute | solution.py:31
  567.5 215.5 %reduce-scatter.9.cloned.1.call-start = ((), (), s32[]{:S(2)}) async-start(), calls=%async_computation.9 | async-start | bytes 1474560 | tf_op jit(solution)/shard_map/reduce_scatter | solution.py:718
  576.6 19.8 %collective-permute-start.108 = (bf16[256,1152]{1,0:T(8,128)(2,1)S(1)}, bf16[256,1152]{1,0:T(8,128)(2,1)S(1)}, u32[]{:S(2)}, u32[]{:S(2)}) collective-permute-start(bf16[256,1152]{1,0:T(8,128)(2,1)S(1)} %get-tuple-element.323.refs_0_.refs_10_), channel_id=1, source_target_pairs={{0,1},{1,0},{2,3},{3,2},{4,5},{5,4},{6,7},{7,6},{8,9},{9,8},{10,11... | collective-permute-start | bytes 1769480 | tf_op jit(solution)/shard_map/ppermute | solution.py:31
  615.2 24.5 %collective-permute-start.117 = (bf16[4,256,1152]{2,1,0:T(8,128)(2,1)}, bf16[4,256,1152]{2,1,0:T(8,128)(2,1)}, u32[]{:S(2)}, u32[]{:S(2)}) collective-permute-start(bf16[4,256,1152]{2,1,0:T(8,128)(2,1)} %get-tuple-element.88), channel_id=1, source_target_pairs={{0,1},{1,0},{2,3},{3,2},{4,5},{5,4},{6,7},{7,6},{8,9},{9,8},{10,11... | collective-permute-start | bytes 7077896 | tf_op jit(solution)/shard_map/ppermute | solution.py:31
  624.8 260.8 %reduce-scatter.11.cloned.1.call-start = ((), (), s32[]{:S(2)}) async-start(), calls=%async_computation.12 | async-start | bytes 1843200 | tf_op jit(solution)/shard_map/reduce_scatter | solution.py:719
  639.6 246.5 %reduce-scatter.17.cloned.1.call-start = ((), (), s32[]{:S(2)}) async-start(), calls=%async_computation.16 | async-start | bytes 1658880 | tf_op jit(solution)/shard_map/reduce_scatter | solution.py:720
  657.4 229.3 %reduce-scatter.15.cloned.1.call-start = ((), (), s32[]{:S(2)}) async-start(), calls=%async_computation.14 | async-start | bytes 1658880 | tf_op jit(solution)/shard_map/reduce_scatter | solution.py:720
  674.9 15.9 %collective-permute-start.125 = (bf16[256,1152]{1,0:T(8,128)(2,1)}, bf16[256,1152]{1,0:T(8,128)(2,1)}, u32[]{:S(2)}, u32[]{:S(2)}) collective-permute-start(bf16[256,1152]{1,0:T(8,128)(2,1)} %get-tuple-element.195.refs_0_.refs_10_), channel_id=1, source_target_pairs={{0,2},{1,3},{2,0},{3,1},{4,6},{5,7},{6,4},{7,5},{8,10},{9,11},{10,... | collective-permute-start | bytes 1769480 | tf_op jit(solution)/shard_map/ppermute | solution.py:31
  675.4 212.0 %all-reduce.16.cloned.1.call-start = ((), (), s32[]{:S(2)}) async-start(), calls=%async_computation.26 | async-start | bytes 1327104 | tf_op jit(solution)/shard_map/psum | solution.py:721
  675.9 23.0 %collective-permute-start.124 = (bf16[256,1152]{1,0:T(8,128)(2,1)}, bf16[256,1152]{1,0:T(8,128)(2,1)S(1)}, u32[]{:S(2)}, u32[]{:S(2)}) collective-permute-start(bf16[256,1152]{1,0:T(8,128)(2,1)} %get-tuple-element.195.refs_0_.refs_10_), channel_id=1, source_target_pairs={{0,1},{1,0},{2,3},{3,2},{4,5},{5,4},{6,7},{7,6},{8,9},{9,8},{10,11... | collective-permute-start | bytes 1769480 | tf_op jit(solution)/shard_map/ppermute | solution.py:31
  744.1 149.7 %all-gather.47.cloned.1.call-start = ((), (), s32[]{:S(2)}) async-start(), calls=%async_computation.23 | async-start | bytes 3317760 | tf_op jit(solution)/shard_map/all_gather | solution.py:724
  744.6 165.8 %all-gather.43.cloned.1.call-start = ((), (), s32[]{:S(2)}) async-start(), calls=%async_computation.21 | async-start | bytes 2654208 | tf_op jit(solution)/shard_map/all_gather | solution.py:722
  774.1 52.2 %collective-permute-start.133 = (bf16[4,256,1152]{2,1,0:T(8,128)(2,1)}, bf16[4,256,1152]{2,1,0:T(8,128)(2,1)}, u32[]{:S(2)}, u32[]{:S(2)}) collective-permute-start(bf16[4,256,1152]{2,1,0:T(8,128)(2,1)} %get-tuple-element.92), channel_id=1, source_target_pairs={{0,1},{1,0},{2,3},{3,2},{4,5},{5,4},{6,7},{7,6},{8,9},{9,8},{10,11... | collective-permute-start | bytes 7077896 | tf_op jit(solution)/shard_map/ppermute | solution.py:31
  783.0 141.6 %all-reduce.14.cloned.1.call-start = ((), (), s32[]{:S(2)}) async-start(), calls=%async_computation.25 | async-start | bytes 147456 | tf_op jit(solution)/shard_map/psum | solution.py:744
  832.6 28.3 %collective-permute-start.137 = (bf16[128,1152]{1,0:T(8,128)(2,1)}, bf16[128,1152]{1,0:T(8,128)(2,1)}, u32[]{:S(2)}, u32[]{:S(2)}) collective-permute-start(bf16[128,1152]{1,0:T(8,128)(2,1)} %get-tuple-element.240), channel_id=1, source_target_pairs={{0,4},{1,5},{2,6},{3,7},{4,0},{5,1},{6,2},{7,3},{8,12},{9,13},{10,... | collective-permute-start | bytes 884744 | tf_op jit(solution)/shard_map/ppermute | solution.py:31
  833.8 27.1 %collective-permute-start.135 = (bf16[128,1152]{1,0:T(8,128)(2,1)}, bf16[128,1152]{1,0:T(8,128)(2,1)}, u32[]{:S(2)}, u32[]{:S(2)}) collective-permute-start(bf16[128,1152]{1,0:T(8,128)(2,1)} %get-tuple-element.241), channel_id=1, source_target_pairs={{0,2},{1,3},{2,0},{3,1},{4,6},{5,7},{6,4},{7,5},{8,10},{9,11},{10,... | collective-permute-start | bytes 884744 | tf_op jit(solution)/shard_map/ppermute | solution.py:31
  857.9 73.7 %reduce-scatter.7.cloned.1.call-start = ((), (), s32[]{:S(2)}) async-start(), calls=%async_computation.8 | async-start | bytes 1474560 | tf_op jit(solution)/shard_map/reduce_scatter | solution.py:718
  868.5 116.3 %all-reduce.12.cloned.1.call-start = ((), (), s32[]{:S(2)}) async-start(), calls=%async_computation.24 | async-start | bytes 884736 | tf_op jit(solution)/shard_map/psum | solution.py:729
  885.5 153.1 %all-gather.45.cloned.1.call-start = ((), (), s32[]{:S(2)}) async-start(), calls=%async_computation.22 | async-start | bytes 3317760 | tf_op jit(solution)/shard_map/all_gather | solution.py:724
  886.1 187.0 %all-gather.35.cloned.1.call-start = ((), (), s32[]{:S(2)}) async-start(), calls=%async_computation.17 | async-start | bytes 2985984 | tf_op jit(solution)/shard_map/all_gather | solution.py:726
  886.6 195.5 %all-gather.33.cloned.1.call-start = ((), (), s32[]{:S(2)}) async-start(), calls=%async_computation.15 | async-start | bytes 2985984 | tf_op jit(solution)/shard_map/all_gather | solution.py:726
  887.4 226.9 %all-gather.31.cloned.1.call-start = ((), (), s32[]{:S(2)}) async-start(), calls=%async_computation.11 | async-start | bytes 2985984 | tf_op jit(solution)/shard_map/all_gather | solution.py:727
  888.0 258.6 %all-gather.29.cloned.1.call-start = ((), (), s32[]{:S(2)}) async-start(), calls=%async_computation.10 | async-start | bytes 2985984 | tf_op jit(solution)/shard_map/all_gather | solution.py:727
  888.7 289.0 %all-gather.41.cloned.1.call-start = ((), (), s32[]{:S(2)}) async-start(), calls=%async_computation.20 | async-start | bytes 2654208 | tf_op jit(solution)/shard_map/all_gather | solution.py:722
  (262 other events, 2563.2 us)
Sparse Core Ops, SparseCore 0:
  19.7 50.7 all-reduce.17
  206.4 34.2 all-gather.24
  242.9 31.8 all-gather.36
  389.5 34.1 all-gather.26
  425.8 31.8 all-gather.38
  567.6 30.9 reduce-scatter.12
  624.9 27.8 reduce-scatter.8
  655.1 32.4 reduce-scatter.10
  690.0 30.5 reduce-scatter.16
  722.8 30.4 reduce-scatter.14
  755.9 40.2 all-reduce.15
  797.9 31.0 all-gather.46
  830.9 28.9 all-gather.42
  862.2 34.5 all-reduce.13
  899.1 29.1 reduce-scatter.6
  931.7 53.1 all-reduce.11
  986.8 30.7 all-gather.44
  1019.5 30.2 all-gather.34
  1051.9 30.2 all-gather.32
  1084.0 30.2 all-gather.30
  1116.3 30.2 all-gather.28
  1148.6 29.0 all-gather.40
